TPU v7x, 32 devices: a whole 2x2x4 slice. The times are simulated.
32 devices in a mesh: band: 8 (over z, x), grid: 4 (over y, core).
Axes of the slice: x: 2, y: 2, z: 4, core: 2. Of those that a mesh axis runs over, the one named last changes fastest.
Arguments:
- trial_bands: float32 [16, 40, 32, 128], P('band', 'grid'), may hold values from -6 to 6
- potential: float32 [40, 32, 128], P('grid'), may hold values from -2 to 0
Outputs:
- filtered: float32 [16, 40, 32, 128], P('band', 'grid')
- projected: float32 [16, 16], P('band')
- residual_norms: float32 [16], P('band')
All inputs are finite; a program needn't handle non-finite values.
Results may differ from a plain program's by a relative error of at most 0.00016.
Values sent between devices are 32-bit elements; how exact they have to be, the bound alone decides.
A program may use at most 64 MiB of HBM per device.

v0:
```python
import jax
import jax.numpy as jnp
from jax import lax
from jax.sharding import PartitionSpec as P

CENTER = 4.25
HALF_WIDTH = 3.75
LOWEST = -2.0
SIGMA_ONE = HALF_WIDTH / (LOWEST - CENTER)
FOUR_THIRDS = 4.0 / 3.0
TWELFTH = 1.0 / 12.0
filter_degree = 4


def padded_2(cells, sides, width):
    for axis, dim in sides:
        count = lax.axis_size(axis)
        head = lax.slice_in_dim(cells, 0, width, axis=dim)
        tail = lax.slice_in_dim(cells, cells.shape[dim] - width, cells.shape[dim], axis=dim)
        cells = jnp.concatenate(
            [
                lax.ppermute(tail, axis, [(i, (i + 1) % count) for i in range(count)]),
                cells,
                lax.ppermute(head, axis, [((i + 1) % count, i) for i in range(count)]),
            ],
            axis=dim,
        )
    return cells


def operate(field_in, potential):
    padded = padded_2(field_in, (("grid", 1),), 2)
    plane_count = field_in.shape[1]
    near_sum = padded[:, 1 : 1 + plane_count] + padded[:, 3 : 3 + plane_count]
    near_sum = near_sum + jnp.roll(field_in, 1, 2) + jnp.roll(field_in, -1, 2)
    near_sum = near_sum + jnp.roll(field_in, 1, 3) + jnp.roll(field_in, -1, 3)
    far_sum = padded[:, 0:plane_count] + padded[:, 4 : 4 + plane_count]
    far_sum = far_sum + jnp.roll(field_in, 2, 2) + jnp.roll(field_in, -2, 2)
    far_sum = far_sum + jnp.roll(field_in, 2, 3) + jnp.roll(field_in, -2, 3)
    kinetic = 0.5 * (7.5 * field_in - FOUR_THIRDS * near_sum + TWELFTH * far_sum)
    return kinetic + potential * field_in


def on_device(trial_bands, potential):
    sigma_now = SIGMA_ONE
    previous = trial_bands
    current = (operate(trial_bands, potential) - CENTER * trial_bands) * (SIGMA_ONE / HALF_WIDTH)
    for repeat_index in range(filter_degree - 1):
        sigma_next = 1.0 / (2.0 / SIGMA_ONE - sigma_now)
        following = (operate(current, potential) - CENTER * current) * (
            2.0 * sigma_next / HALF_WIDTH
        ) - sigma_now * sigma_next * previous
        previous, current, sigma_now = (current, following, sigma_next)
    applied = operate(current, potential)
    band_count = current.shape[0]
    flat_bands = current.reshape(band_count, -1)
    flat_image = applied.reshape(band_count, -1)
    cell_total = flat_bands.shape[1] * lax.axis_size("grid")
    inverse_cells = 1.0 / cell_total
    bands_all = band_count * lax.axis_size("band")
    first_band = lax.axis_index("band") * band_count
    local_norms = jnp.sum(flat_image * flat_image, axis=1)
    cell_bands, cell_image = (
        lax.all_to_all(flat_bands, "band", split_axis=1, concat_axis=0, tiled=True),
        lax.all_to_all(flat_image, "band", split_axis=1, concat_axis=0, tiled=True),
    )
    margin_part = jnp.dot(
        cell_bands,
        cell_bands.T,
        precision=lax.Precision.HIGHEST,
        preferred_element_type=jnp.float32,
    )
    image_part = jnp.dot(
        cell_image,
        cell_bands.T,
        precision=lax.Precision.HIGHEST,
        preferred_element_type=jnp.float32,
    )
    norm_full = lax.dynamic_update_slice(
        jnp.zeros((bands_all,), jnp.float32), local_norms, (first_band,)
    )
    margin, subspace, image_norms = lax.psum((margin_part, image_part, norm_full), ("band", "grid"))
    margin = margin * inverse_cells
    subspace = subspace * inverse_cells
    image_norms = image_norms * inverse_cells
    factor = jnp.linalg.cholesky(margin)
    coefficients = lax.linalg.triangular_solve(factor, subspace.T, left_side=True, lower=True)
    projected = lax.linalg.triangular_solve(factor, coefficients.T, left_side=True, lower=True)
    residual_norms = image_norms - jnp.sum(coefficients * coefficients, axis=0)
    projected_rows = lax.dynamic_slice_in_dim(projected, first_band, band_count, 0)
    residual_rows = lax.dynamic_slice_in_dim(residual_norms, first_band, band_count, 0)
    return (current, projected_rows, residual_rows)


def solution(mesh):
    in_specs = (P("band", "grid", None, None), P("grid", None, None))
    out_specs = (P("band", "grid", None, None), P("band", None), P("band"))
    return jax.shard_map(
        on_device, mesh=mesh, in_specs=in_specs, out_specs=out_specs, check_vma=False
    )
```

profile of v0, /device:TPU:0, one launch (start us, length us, event | category | flops | bytes accessed | tf_op | source)
XLA Modules:
  0.0 107.2 jit_solution(2089261270580280217)
XLA Ops:
  0.6 0.9 fusion.149
  1.5 0.5 collective-permute-start
  2.0 2.0 %collective-permute-start.1 = (f32[2,2,32,128]{3,2,1,0:T(8,128)S(1)}, f32[2,2,32,128]{3,2,1,0:T(8,128)S(1)}, u32[]{:S(2)}, u32[]{:S(2)}) collective-permute-start(f32[2,2,32,128]{3,2,1,0:T(8,128)S(1)} %get-tuple-element.94), channel_id=1, source_target_pairs={{1,0},{2,1},{3,2},{0,3},{5,4},{6,5},{7,6},{4,7},{9,8},{10,9},{11,1... | collective-permute-start | bytes 196616 | tf_op jit(solution)/shard_map/ppermute | solution.py:24
  4.1 1.2 %fusion.152 = (f32[2,10,32,2]{3,2,1,0:T(8,128)S(1)}, f32[2,10,32,2]{3,2,1,0:T(8,128)S(1)}) fusion(f32[2,10,32,128]{3,2,1,0:T(8,128)} %param.4), kind=kLoop, calls=%fused_computation.193 | loop fusion | bytes 20480 | tf_op jit(solution)/shard_map/jit(_roll_static)/slice | solution.py:39
  5.9 0.8 copy-done.2
  6.9 0.7 broadcast_multiply_fusion
  8.4 1.5 %collective-permute-start.2 = (f32[2,2,32,128]{3,2,1,0:T(8,128)S(1)}, f32[2,2,32,128]{3,2,1,0:T(8,128)S(1)}, u32[]{:S(2)}, u32[]{:S(2)}) collective-permute-start(f32[2,2,32,128]{3,2,1,0:T(8,128)S(1)} %get-tuple-element.81), channel_id=1, source_target_pairs={{0,1},{1,2},{2,3},{3,0},{4,5},{5,6},{6,7},{7,4},{8,9},{9,10},{10,1... | collective-permute-start | bytes 196616 | tf_op jit(solution)/shard_map/ppermute | solution.py:22
  9.9 0.3 collective-permute-start.3
  10.3 1.9 %collective-permute-done.2 = f32[2,2,32,128]{3,2,1,0:T(8,128)S(1)} collective-permute-done((f32[2,2,32,128]{3,2,1,0:T(8,128)S(1)}, f32[2,2,32,128]{3,2,1,0:T(8,128)S(1)}, u32[]{:S(2)}, u32[]{:S(2)}) %collective-permute-start.2) | collective-permute-done | bytes 65568 | tf_op jit(solution)/shard_map/ppermute | solution.py:22
  12.2 0.5 collective-permute-done.3
  12.6 0.7 fusion.55
  14.2 1.9 %collective-permute-start.4 = (f32[2,2,32,128]{3,2,1,0:T(8,128)S(1)}, f32[2,2,32,128]{3,2,1,0:T(8,128)S(1)}, u32[]{:S(2)}, u32[]{:S(2)}) collective-permute-start(f32[2,2,32,128]{3,2,1,0:T(8,128)S(1)} %get-tuple-element.63), channel_id=1, source_target_pairs={{0,1},{1,2},{2,3},{3,0},{4,5},{5,6},{6,7},{7,4},{8,9},{9,10},{10,1... | collective-permute-start | bytes 196616 | tf_op jit(solution)/shard_map/ppermute | solution.py:22
  16.1 0.3 collective-permute-start.5
  16.4 1.9 %collective-permute-done.4 = f32[2,2,32,128]{3,2,1,0:T(8,128)S(1)} collective-permute-done((f32[2,2,32,128]{3,2,1,0:T(8,128)S(1)}, f32[2,2,32,128]{3,2,1,0:T(8,128)S(1)}, u32[]{:S(2)}, u32[]{:S(2)}) %collective-permute-start.4) | collective-permute-done | bytes 65568 | tf_op jit(solution)/shard_map/ppermute | solution.py:22
  18.3 0.2 collective-permute-done.5
  18.5 0.6 fusion.40
  20.0 1.9 %collective-permute-start.6 = (f32[2,2,32,128]{3,2,1,0:T(8,128)S(1)}, f32[2,2,32,128]{3,2,1,0:T(8,128)S(1)}, u32[]{:S(2)}, u32[]{:S(2)}) collective-permute-start(f32[2,2,32,128]{3,2,1,0:T(8,128)S(1)} %get-tuple-element.45), channel_id=1, source_target_pairs={{0,1},{1,2},{2,3},{3,0},{4,5},{5,6},{6,7},{7,4},{8,9},{9,10},{10,1... | collective-permute-start | bytes 196616 | tf_op jit(solution)/shard_map/ppermute | solution.py:22
  22.1 1.9 %collective-permute-done.6 = f32[2,2,32,128]{3,2,1,0:T(8,128)S(1)} collective-permute-done((f32[2,2,32,128]{3,2,1,0:T(8,128)S(1)}, f32[2,2,32,128]{3,2,1,0:T(8,128)S(1)}, u32[]{:S(2)}, u32[]{:S(2)}) %collective-permute-start.6) | collective-permute-done | bytes 65568 | tf_op jit(solution)/shard_map/ppermute | solution.py:22
  23.9 0.2 collective-permute-done.7
  24.2 0.6 fusion.25
  25.3 0.8 fusion.116
  26.2 0.9 fusion.117
  27.1 0.6 fusion.113
  27.7 0.8 all_to_all.28
  28.5 1.9 %copy.7 = f32[2,8,5120]{2,0,1:T(2,128)} copy(f32[2,8,5120]{2,1,0:T(8,128)} %all_to_all.28) | data formatting | bytes 655360 | tf_op jit(solution)/shard_map/all_to_all | solution.py:64
  30.4 5.1 %all-to-all-start = ((f32[2,8,5120]{2,0,1:T(2,128)}), f32[2,8,5120]{2,0,1:T(2,128)}, u32[]{:S(2)}, u32[]{:S(2)}) async-start(f32[2,8,5120]{2,0,1:T(2,128)} %copy.7), calls=%async_computation | async-start | bytes 655360 | tf_op jit(solution)/shard_map/all_to_all | solution.py:64
  35.6 0.8 copy-done.3
  36.4 1.4 %collective-permute-start.8 = (f32[2,2,32,128]{3,2,1,0:T(8,128)S(1)}, f32[2,2,32,128]{3,2,1,0:T(8,128)S(1)}, u32[]{:S(2)}, u32[]{:S(2)}) collective-permute-start(f32[2,2,32,128]{3,2,1,0:T(8,128)S(1)} %copy-done.3), channel_id=1, source_target_pairs={{0,1},{1,2},{2,3},{3,0},{4,5},{5,6},{6,7},{7,4},{8,9},{9,10},{10,1... | collective-permute-start | bytes 196616 | tf_op jit(solution)/shard_map/ppermute | solution.py:22
  37.8 0.4 collective-permute-start.9
  38.2 1.9 %collective-permute-done.8 = f32[2,2,32,128]{3,2,1,0:T(8,128)S(1)} collective-permute-done((f32[2,2,32,128]{3,2,1,0:T(8,128)S(1)}, f32[2,2,32,128]{3,2,1,0:T(8,128)S(1)}, u32[]{:S(2)}, u32[]{:S(2)}) %collective-permute-start.8) | collective-permute-done | bytes 65568 | tf_op jit(solution)/shard_map/ppermute | solution.py:22
  40.1 2.4 %multiply_reduce_fusion = (f32[2]{0:T(128)S(1)}, f32[2,10,32,128]{3,2,1,0:T(8,128)}) fusion(f32[2,10,32,128]{3,2,1,0:T(8,128)S(1)} %fusion.25, f32[10,32,128]{2,1,0:T(8,128)S(1)} %copy-done.2, f32[2,10,32,2]{3,2,1,0:T(8,128)} %get-tuple-element.26, f32[2,10,32,126]{3,2,1,0:T(8,128)} %get-tuple-element.28, f32[2,10,32,126]{3,2,1,0:T(8,128)} %get-tuple-element.27, ...), kind=kLoop, calls=%fused_computation.122 | loop fusion | flops 2621438 | bytes 3571720 | tf_op jit(solution)/shard_map/reduce_sum | solution.py:62
  42.5 1.0 all_to_all.32
  43.6 1.0 copy.10
  44.6 2.4 %all-to-all-done = f32[2,8,5120]{2,0,1:T(2,128)} async-done(((f32[2,8,5120]{2,0,1:T(2,128)}), f32[2,8,5120]{2,0,1:T(2,128)}, u32[]{:S(2)}, u32[]{:S(2)}) %all-to-all-start) | async-done | bytes 327712 | tf_op jit(solution)/shard_map/all_to_all | solution.py:64
  47.0 3.9 %all-to-all-start.1 = ((f32[2,8,5120]{2,0,1:T(2,128)}), f32[2,8,5120]{2,0,1:T(2,128)S(1)}, u32[]{:S(2)}, u32[]{:S(2)}) async-start(f32[2,8,5120]{2,0,1:T(2,128)} %copy.10), calls=%async_computation.1 | async-start | bytes 655360 | tf_op jit(solution)/shard_map/all_to_all | solution.py:65
  50.9 0.2 dynamic_update_slice.3
  51.2 1.2 %all_to_all.31 = f32[16,5120]{1,0:T(8,128)S(1)} reshape(f32[8,2,5120]{2,1,0:T(2,128)} %bitcast) | data formatting | bytes 655360 | tf_op jit(solution)/shard_map/all_to_all | solution.py:64
  52.4 0.5 fusion.154
  52.9 9.4 %all-to-all-done.1 = f32[2,8,5120]{2,0,1:T(2,128)S(1)} async-done(((f32[2,8,5120]{2,0,1:T(2,128)}), f32[2,8,5120]{2,0,1:T(2,128)S(1)}, u32[]{:S(2)}, u32[]{:S(2)}) %all-to-all-start.1) | async-done | bytes 327712 | tf_op jit(solution)/shard_map/all_to_all | solution.py:65
  62.5 0.5 fusion.155
  63.1 38.4 %all-reduce = (f32[16,16]{0,1:T(8,128)S(1)}, f32[16,16]{0,1:T(8,128)S(1)}, f32[16]{0:T(128)S(1)}) all-reduce(f32[16,16]{0,1:T(8,128)S(1)} %fusion.154, f32[16,16]{0,1:T(8,128)S(1)} %fusion.155, f32[16]{0:T(128)S(1)} %dynamic_update_slice.3), channel_id=1, replica_groups=mesh['band'=8,'grid'=4] {'band','grid'}, use_global_device_ids=true, to_apply=%region_0.1 | all-reduce | flops 528 | bytes 4224 | tf_op jit(solution)/shard_map/psum | solution.py:82
  101.5 1.5 %cholesky.18 = f32[16,16]{1,0:T(8,128)S(1)} custom-call(f32[16,16]{1,0:T(8,128)S(1)} %fusion.103), custom_call_target="Cholesky" | custom-call | tf_op jit(solution)/shard_map/jit(cholesky)/cholesky | solution.py:86
  103.0 0.6 compare_reduce_fusion
  103.7 0.6 fusion.96
  104.3 1.2 %custom-call.8 = f32[1,16,16]{1,2,0:T(8,128)S(1)} custom-call(f32[1,16,16]{2,1,0:T(8,128)S(1)} %fusion.96), custom_call_target="InvertDiagBlocksLowerTriangular" | custom-call | tf_op jit(solution)/shard_map/triangular_solve/custom-call.0 | solution.py:88
  105.6 0.2 multiply_reduce_fusion.1
  105.8 0.6 dynamic_slice.7
  106.6 0.6 constant_dynamic-slice_fusion
  (62 shorter events, 4.3 us)
Async XLA Ops:
  1.5 5.3 %collective-permute-start = (f32[2,2,32,128]{3,2,1,0:T(8,128)S(1)}, f32[2,2,32,128]{3,2,1,0:T(8,128)S(1)}, u32[]{:S(2)}, u32[]{:S(2)}) collective-permute-start(f32[2,2,32,128]{3,2,1,0:T(8,128)S(1)} %get-tuple-element.93), channel_id=1, source_target_pairs={{0,1},{1,2},{2,3},{3,0},{4,5},{5,6},{6,7},{7,4},{8,9},{9,10},{10,1... | collective-permute-start | bytes 196616 | tf_op jit(solution)/shard_map/ppermute | solution.py:22
  2.0 3.3 %copy-start = (f32[2,10,32,128]{3,2,1,0:T(8,128)S(1)}, f32[2,10,32,128]{3,2,1,0:T(8,128)}, u32[]{:S(2)}) copy-start(f32[2,10,32,128]{3,2,1,0:T(8,128)} %param.4) | copy-start | bytes 983044
  2.0 4.9 %collective-permute-start.1 = (f32[2,2,32,128]{3,2,1,0:T(8,128)S(1)}, f32[2,2,32,128]{3,2,1,0:T(8,128)S(1)}, u32[]{:S(2)}, u32[]{:S(2)}) collective-permute-start(f32[2,2,32,128]{3,2,1,0:T(8,128)S(1)} %get-tuple-element.94), channel_id=1, source_target_pairs={{1,0},{2,1},{3,2},{0,3},{5,4},{6,5},{7,6},{4,7},{9,8},{10,9},{11,1... | collective-permute-start | bytes 196616 | tf_op jit(solution)/shard_map/ppermute | solution.py:24
  5.8 0.9 copy-start.2
  8.4 3.7 %collective-permute-start.2 = (f32[2,2,32,128]{3,2,1,0:T(8,128)S(1)}, f32[2,2,32,128]{3,2,1,0:T(8,128)S(1)}, u32[]{:S(2)}, u32[]{:S(2)}) collective-permute-start(f32[2,2,32,128]{3,2,1,0:T(8,128)S(1)} %get-tuple-element.81), channel_id=1, source_target_pairs={{0,1},{1,2},{2,3},{3,0},{4,5},{5,6},{6,7},{7,4},{8,9},{9,10},{10,1... | collective-permute-start | bytes 196616 | tf_op jit(solution)/shard_map/ppermute | solution.py:22
  9.9 2.7 %collective-permute-start.3 = (f32[2,2,32,128]{3,2,1,0:T(8,128)S(1)}, f32[2,2,32,128]{3,2,1,0:T(8,128)S(1)}, u32[]{:S(2)}, u32[]{:S(2)}) collective-permute-start(f32[2,2,32,128]{3,2,1,0:T(8,128)S(1)} %get-tuple-element.82), channel_id=1, source_target_pairs={{1,0},{2,1},{3,2},{0,3},{5,4},{6,5},{7,6},{4,7},{9,8},{10,9},{11,1... | collective-permute-start | bytes 196616 | tf_op jit(solution)/shard_map/ppermute | solution.py:24
  14.2 4.1 %collective-permute-start.4 = (f32[2,2,32,128]{3,2,1,0:T(8,128)S(1)}, f32[2,2,32,128]{3,2,1,0:T(8,128)S(1)}, u32[]{:S(2)}, u32[]{:S(2)}) collective-permute-start(f32[2,2,32,128]{3,2,1,0:T(8,128)S(1)} %get-tuple-element.63), channel_id=1, source_target_pairs={{0,1},{1,2},{2,3},{3,0},{4,5},{5,6},{6,7},{7,4},{8,9},{9,10},{10,1... | collective-permute-start | bytes 196616 | tf_op jit(solution)/shard_map/ppermute | solution.py:22
  16.1 2.4 %collective-permute-start.5 = (f32[2,2,32,128]{3,2,1,0:T(8,128)S(1)}, f32[2,2,32,128]{3,2,1,0:T(8,128)S(1)}, u32[]{:S(2)}, u32[]{:S(2)}) collective-permute-start(f32[2,2,32,128]{3,2,1,0:T(8,128)S(1)} %get-tuple-element.64), channel_id=1, source_target_pairs={{1,0},{2,1},{3,2},{0,3},{5,4},{6,5},{7,6},{4,7},{9,8},{10,9},{11,1... | collective-permute-start | bytes 196616 | tf_op jit(solution)/shard_map/ppermute | solution.py:24
  20.0 3.9 %collective-permute-start.6 = (f32[2,2,32,128]{3,2,1,0:T(8,128)S(1)}, f32[2,2,32,128]{3,2,1,0:T(8,128)S(1)}, u32[]{:S(2)}, u32[]{:S(2)}) collective-permute-start(f32[2,2,32,128]{3,2,1,0:T(8,128)S(1)} %get-tuple-element.45), channel_id=1, source_target_pairs={{0,1},{1,2},{2,3},{3,0},{4,5},{5,6},{6,7},{7,4},{8,9},{9,10},{10,1... | collective-permute-start | bytes 196616 | tf_op jit(solution)/shard_map/ppermute | solution.py:22
  22.0 2.2 %collective-permute-start.7 = (f32[2,2,32,128]{3,2,1,0:T(8,128)S(1)}, f32[2,2,32,128]{3,2,1,0:T(8,128)S(1)}, u32[]{:S(2)}, u32[]{:S(2)}) collective-permute-start(f32[2,2,32,128]{3,2,1,0:T(8,128)S(1)} %get-tuple-element.46), channel_id=1, source_target_pairs={{1,0},{2,1},{3,2},{0,3},{5,4},{6,5},{7,6},{4,7},{9,8},{10,9},{11,1... | collective-permute-start | bytes 196616 | tf_op jit(solution)/shard_map/ppermute | solution.py:24
  24.8 15.2 %copy-start.1 = (f32[2,10,32,128]{3,2,1,0:T(8,128)}, f32[2,10,32,128]{3,2,1,0:T(8,128)S(1)}, u32[]{:S(2)}) copy-start(f32[2,10,32,128]{3,2,1,0:T(8,128)S(1)} %fusion.25) | copy-start | bytes 983044
  30.4 16.6 %all-to-all-start = ((f32[2,8,5120]{2,0,1:T(2,128)}), f32[2,8,5120]{2,0,1:T(2,128)}, u32[]{:S(2)}, u32[]{:S(2)}) async-start(f32[2,8,5120]{2,0,1:T(2,128)} %copy.7), calls=%async_computation | async-start | bytes 655360 | tf_op jit(solution)/shard_map/all_to_all | solution.py:64
  35.5 0.8 copy-start.3
  36.4 3.7 %collective-permute-start.8 = (f32[2,2,32,128]{3,2,1,0:T(8,128)S(1)}, f32[2,2,32,128]{3,2,1,0:T(8,128)S(1)}, u32[]{:S(2)}, u32[]{:S(2)}) collective-permute-start(f32[2,2,32,128]{3,2,1,0:T(8,128)S(1)} %copy-done.3), channel_id=1, source_target_pairs={{0,1},{1,2},{2,3},{3,0},{4,5},{5,6},{6,7},{7,4},{8,9},{9,10},{10,1... | collective-permute-start | bytes 196616 | tf_op jit(solution)/shard_map/ppermute | solution.py:22
  37.8 2.3 %collective-permute-start.9 = (f32[2,2,32,128]{3,2,1,0:T(8,128)S(1)}, f32[2,2,32,128]{3,2,1,0:T(8,128)S(1)}, u32[]{:S(2)}, u32[]{:S(2)}) collective-permute-start(f32[2,2,32,128]{3,2,1,0:T(8,128)S(1)} %get-tuple-element.20), channel_id=1, source_target_pairs={{1,0},{2,1},{3,2},{0,3},{5,4},{6,5},{7,6},{4,7},{9,8},{10,9},{11,1... | collective-permute-start | bytes 196616 | tf_op jit(solution)/shard_map/ppermute | solution.py:24
  47.0 15.3 %all-to-all-start.1 = ((f32[2,8,5120]{2,0,1:T(2,128)}), f32[2,8,5120]{2,0,1:T(2,128)S(1)}, u32[]{:S(2)}, u32[]{:S(2)}) async-start(f32[2,8,5120]{2,0,1:T(2,128)} %copy.10), calls=%async_computation.1 | async-start | bytes 655360 | tf_op jit(solution)/shard_map/all_to_all | solution.py:65
where the time goes:
time: 108 us; the launch traced here: 107 us
  blocking collectives  38.4 us (36%)
  waiting for transfers between devices  20.3 us (19%)
  starting transfers between devices  19.4 us (18%)
  local copies, waits for them, and re-layouts  17.5 us (16%)
  other arithmetic  9.13 us (8%)
  matrix products  1.5 us (1%)
    psum x1, blocking collectives, on_device(): lax.psum((margin_part, image_part, norm_full), ('band', 'grid'))  38.4 us
    all_to_all x1, waiting for transfers between devices, on_device(): lax.all_to_all(flat_image, 'band', split_axis=1, concat_axis=0, tiled=True)  9.35 us
    ppermute x5, waiting for transfers between devices, padded_2(): lax.ppermute(tail, axis, [(i, (i + 1) % count) for i in range(count)])  7.58 us
    ppermute x5, starting transfers between devices, padded_2(): lax.ppermute(tail, axis, [(i, (i + 1) % count) for i in range(count)])  7.26 us
    all_to_all x1, starting transfers between devices, on_device(): lax.all_to_all(flat_bands, 'band', split_axis=1, concat_axis=0, tiled=True)  5.1 us
    slice x10, local copies, waits for them, and re-layouts, operate(): far_sum = far_sum + jnp.roll(field_in, 2, 3) + jnp.roll(field_in, -2, 3)  4.15 us
    all_to_all x1, starting transfers between devices, on_device(): lax.all_to_all(flat_image, 'band', split_axis=1, concat_axis=0, tiled=True)  3.94 us
    all_to_all x3, local copies, waits for them, and re-layouts, on_device(): lax.all_to_all(flat_bands, 'band', split_axis=1, concat_axis=0, tiled=True)  3.91 us
  transfers between devices with their start and end apart: 12, of which 9 were waited for; matrix products, arithmetic and copies ran while one was open for 6% of the time, Pallas kernels for 0%

commit v1 on v0

v1 whole, which is shorter than its diff:
```python
import functools

import jax
import jax.numpy as jnp
from jax import lax
from jax.experimental import pallas as pl
from jax.experimental.pallas import tpu as pltpu
from jax.sharding import PartitionSpec as P

CENTER = 4.25
HALF_WIDTH = 3.75
LOWEST = -2.0
SIGMA_ONE = HALF_WIDTH / (LOWEST - CENTER)
MESH = pl.DeviceIdType.MESH
HIGHEST = lax.Precision.HIGHEST
CONTRACT_LANES = (((1,), (1,)), ((), ()))


def filter_steps():
    sigma_now = SIGMA_ONE
    steps = [(SIGMA_ONE / HALF_WIDTH, 0.0)]
    for _ in range(3):
        sigma_next = 1.0 / (2.0 / SIGMA_ONE - sigma_now)
        steps.append((2.0 * sigma_next / HALF_WIDTH, sigma_now * sigma_next))
        sigma_now = sigma_next
    return steps


def kernel(
    sizes,
    x_hbm,
    v_hbm,
    f_out,
    projected_out,
    residual_out,
    x0,
    vp,
    y1,
    y2,
    y3,
    y4,
    image,
    f_share,
    f_all,
    h_all,
    part_a,
    part_b,
    halo_send,
    halo_recv,
    f_send,
    f_recv,
    h_send,
    h_recv,
    a_send,
    a_recv,
    b_send,
    b_recv,
    local_sem,
):
    nb, nz, nx, n_band, n_grid, share, width, cells = sizes
    rows = nz * nx
    bands = nb * n_band
    me = lax.axis_index("band")
    slab = lax.axis_index("grid")
    right = lax.rem(slab + 1, n_grid)
    left = lax.rem(slab + n_grid - 1, n_grid)
    ny = x0.shape[-1]

    own = [
        pltpu.make_async_copy(x_hbm, x0.at[:, pl.ds(4 * nx, rows)], local_sem.at[0]),
        pltpu.make_async_copy(v_hbm, vp.at[pl.ds(2 * nx, rows)], local_sem.at[1]),
    ]
    for copy in own:
        copy.start()

    barrier = pltpu.get_barrier_semaphore()

    def greet_band(d, carry):
        pl.semaphore_signal(
            barrier, inc=1, device_id=(lax.rem(me + d, n_band), slab), device_id_type=MESH
        )
        return carry

    def greet_grid(d, carry):
        pl.semaphore_signal(
            barrier, inc=1, device_id=(me, lax.rem(slab + d, n_grid)), device_id_type=MESH
        )
        return carry

    lax.fori_loop(1, n_grid, greet_grid, 0)
    lax.fori_loop(1, n_band, greet_band, 0)
    pl.semaphore_wait(barrier, n_band + n_grid - 2)

    def halo_copy(index, src, dst, to):
        return pltpu.make_async_remote_copy(
            src_ref=src,
            dst_ref=dst,
            send_sem=halo_send.at[index],
            recv_sem=halo_recv.at[index],
            device_id=(me, to),
            device_id_type=MESH,
        )

    def up(index, src, first, dst, depth):
        return halo_copy(
            index,
            src.at[:, pl.ds((first + nz - depth) * nx, depth * nx)],
            dst.at[:, pl.ds(0, depth * nx)],
            right,
        )

    def down(index, src, first, dst, depth):
        return halo_copy(
            index,
            src.at[:, pl.ds(first * nx, depth * nx)],
            dst.at[:, pl.ds((nz + depth) * nx, depth * nx)],
            left,
        )

    swap_x = [up(0, x_hbm, 0, x0, 4), down(1, x_hbm, 0, x0, 4)]
    swap_v = [
        halo_copy(2, v_hbm.at[pl.ds((nz - 2) * nx, 2 * nx)], vp.at[pl.ds(0, 2 * nx)], right),
        halo_copy(3, v_hbm.at[pl.ds(0, 2 * nx)], vp.at[pl.ds((nz + 2) * nx, 2 * nx)], left),
    ]
    swap_2 = [up(4, y2, 4, y2, 4), down(5, y2, 4, y2, 4)]
    swap_4 = [up(6, y4, 2, y4, 2), down(7, y4, 2, y4, 2)]
    for copy in swap_x + swap_v:
        copy.start()

    steps = filter_steps()

    def planes(lo, hi, src, src_halo, dsts, scale, center, prev=None, prev_halo=0, weight=0.0):
        def at(ref, band, halo, plane):
            return ref[band, pl.ds(pl.multiple_of((plane + halo) * nx, nx), nx), :]

        def body(pair, carry):
            first = lo + 2 * pair
            for plane in (first, first + 1):
                local = vp[pl.ds(pl.multiple_of((plane + 2) * nx, nx), nx), :]
                local = (local + (3.75 - center)) * scale
                for band in range(nb):
                    here = at(src, band, src_halo, plane)
                    near = at(src, band, src_halo, plane - 1) + at(src, band, src_halo, plane + 1)
                    far = at(src, band, src_halo, plane - 2) + at(src, band, src_halo, plane + 2)
                    near += pltpu.roll(here, 1, 0) + pltpu.roll(here, nx - 1, 0)
                    far += pltpu.roll(here, 2, 0) + pltpu.roll(here, nx - 2, 0)
                    near += pltpu.roll(here, 1, 1) + pltpu.roll(here, ny - 1, 1)
                    far += pltpu.roll(here, 2, 1) + pltpu.roll(here, ny - 2, 1)
                    value = local * here - near * (scale * 2.0 / 3.0) + far * (scale / 24.0)
                    if prev is not None:
                        value = value - weight * at(prev, band, prev_halo, plane)
                    for dst, halo in dsts:
                        dst[band, pl.ds(pl.multiple_of((plane + halo) * nx, nx), nx), :] = value
            return carry

        lax.fori_loop(0, (hi - lo) // 2, body, 0)

    for copy in own:
        copy.wait()

    step_1 = functools.partial(planes, src=x0, src_halo=4, dsts=[(y1, 2)], scale=steps[0][0], center=CENTER)
    step_1(2, nz - 2)
    for copy in swap_x + swap_v:
        copy.wait()
    step_1(-2, 2)
    step_1(nz - 2, nz + 2)

    step_2 = functools.partial(
        planes, src=y1, src_halo=2, dsts=[(y2, 4)], scale=steps[1][0], center=CENTER,
        prev=x0, prev_halo=4, weight=steps[1][1],
    )
    step_2(0, 4)
    swap_2[1].start()
    step_2(nz - 4, nz)
    swap_2[0].start()
    step_2(4, nz - 4)

    step_3 = functools.partial(
        planes, src=y2, src_halo=4, dsts=[(y3, 2)], scale=steps[2][0], center=CENTER,
        prev=y1, prev_halo=2, weight=steps[2][1],
    )
    step_3(2, nz - 2)
    for copy in swap_2:
        copy.wait()
    step_3(-2, 2)
    step_3(nz - 2, nz + 2)

    step_4 = functools.partial(
        planes, src=y3, src_halo=2, dsts=[(y4, 2), (f_share, 0)], scale=steps[3][0], center=CENTER,
        prev=y2, prev_halo=4, weight=steps[3][1],
    )
    step_4(0, 2)
    swap_4[1].start()
    step_4(nz - 2, nz)
    swap_4[0].start()
    step_4(2, nz - 2)

    padded = share * n_band
    if padded != rows:
        f_share[:, rows:, :] = jnp.zeros((nb, padded - rows, ny), jnp.float32)
        image[:, rows:, :] = jnp.zeros((nb, padded - rows, ny), jnp.float32)

    def to_band(src, dst, send, recv, d):
        partner = lax.rem(me + d, n_band)
        return pltpu.make_async_remote_copy(
            src_ref=src.at[:, pl.ds(pl.multiple_of(partner * share, 8), share)],
            dst_ref=dst.at[me],
            send_sem=send.at[d],
            recv_sem=recv.at[n_band - d],
            device_id=(partner, slab),
            device_id_type=MESH,
        )

    def start_band(src, dst, send, recv):
        def body(d, carry):
            to_band(src, dst, send, recv, d).start()
            return carry

        lax.fori_loop(1, n_band, body, 0)

    def wait_band(src, dst, send, recv):
        def body(d, carry):
            to_band(src, dst, send, recv, d).wait()
            return carry

        lax.fori_loop(1, n_band, body, 0)

    start_band(f_share, f_all, f_send, f_recv)
    out_copy = pltpu.make_async_copy(f_share.at[:, pl.ds(0, rows)], f_out, local_sem.at[2])
    out_copy.start()

    last = functools.partial(planes, src=y4, src_halo=2, dsts=[(image, 0)], scale=1.0, center=0.0)
    last(2, nz - 2)
    for copy in swap_4:
        copy.wait()
    last(0, 2)
    last(nz - 2, nz)
    start_band(image, h_all, h_send, h_recv)

    own_rows = pl.ds(pl.multiple_of(me * share, 8), share)
    f_all[me] = f_share[:, own_rows, :]
    h_all[me] = image[:, own_rows, :]

    def on_lanes(ref):
        whole = ref[...]
        tiles = [
            whole[:, :, 8 * t : 8 * t + 8, :].reshape(bands * 8, ny) for t in range(share // 8)
        ]
        return jnp.concatenate(tiles, axis=1)

    stretched = bands * 8
    same = (
        lax.broadcasted_iota(jnp.int32, (stretched, stretched), 0) % 8
        == lax.broadcasted_iota(jnp.int32, (stretched, stretched), 1) % 8
    )
    column = lax.broadcasted_iota(jnp.int32, (stretched, width), 0) // 8
    lane = lax.broadcasted_iota(jnp.int32, (stretched, width), 1)

    def folded(gram, offset):
        gram = jnp.where(same, gram, 0.0).reshape(bands, 8, stretched).sum(axis=1)
        pick = jnp.where(column + offset == lane, 1.0, 0.0)
        return jnp.dot(gram, pick, precision=HIGHEST, preferred_element_type=jnp.float32)

    wait_band(f_share, f_all, f_send, f_recv)
    filtered = on_lanes(f_all)
    margin = lax.dot_general(
        filtered, filtered, CONTRACT_LANES, precision=HIGHEST, preferred_element_type=jnp.float32
    )
    top = folded(margin, 0)
    wait_band(image, h_all, h_send, h_recv)
    images = on_lanes(h_all)
    mixed = lax.dot_general(
        filtered, images, CONTRACT_LANES, precision=HIGHEST, preferred_element_type=jnp.float32
    )
    top = top + folded(mixed, bands)
    whole = h_all[...]
    squares = (whole * whole).sum(axis=2).reshape(bands, ny)
    norms = lax.dot_general(
        jnp.ones((8, ny), jnp.float32),
        squares,
        CONTRACT_LANES,
        precision=HIGHEST,
        preferred_element_type=jnp.float32,
    )
    part_a[me, 0:bands, :] = top
    part_a[me, bands:, :] = jnp.zeros((8, width), jnp.float32)
    part_a[me, bands:, 0:bands] = norms

    def sum_over(part, count, here, target, send, recv):
        def copy(d):
            return pltpu.make_async_remote_copy(
                src_ref=part.at[here],
                dst_ref=part.at[here],
                send_sem=send.at[d],
                recv_sem=recv.at[count - d],
                device_id=target(lax.rem(here + d, count)),
                device_id_type=MESH,
            )

        def start(d, carry):
            copy(d).start()
            return carry

        def wait(d, carry):
            copy(d).wait()
            return carry

        lax.fori_loop(1, count, start, 0)
        lax.fori_loop(1, count, wait, 0)
        return jnp.sum(part[...], axis=0)

    part_b[slab] = sum_over(part_a, n_band, me, lambda j: (j, slab), a_send, a_recv)
    total = sum_over(part_b, n_grid, slab, lambda j: (me, j), b_send, b_recv) * (1.0 / cells)

    row_of = lax.broadcasted_iota(jnp.int32, (bands, width), 0)
    lane_of = lax.broadcasted_iota(jnp.int32, (bands, width), 1)
    work = total[0:bands]
    work = jnp.where(lane_of == row_of + 2 * bands, 1.0, work)
    for k in range(bands):
        pivot = work[k : k + 1, k : k + 1]
        inverse = lax.rsqrt(pivot)
        inverse = inverse * (1.5 - 0.5 * pivot * inverse * inverse)
        row = work[k : k + 1, :] * inverse
        factor_column = work[:, k : k + 1] * inverse
        below = work - factor_column * row
        work = jnp.where(row_of > k, below, jnp.where(row_of == k, row, work))
    coefficients = jnp.where(lane_of < bands, pltpu.roll(work, width - bands, 1), 0.0)
    inverse_factor = jnp.where(lane_of < bands, pltpu.roll(work, width - 2 * bands, 1), 0.0)
    projected = lax.dot_general(
        inverse_factor,
        coefficients,
        CONTRACT_LANES,
        precision=HIGHEST,
        preferred_element_type=jnp.float32,
    )
    residual = total[bands : bands + 1] - jnp.sum(coefficients * coefficients, axis=0, keepdims=True)
    square_rows = lax.broadcasted_iota(jnp.int32, (bands, bands), 0)
    for r in range(nb):
        mine = me * nb + r
        projected_out[r : r + 1, :] = jnp.sum(
            jnp.where(square_rows == mine, projected, 0.0), axis=0, keepdims=True
        )
        residual_out[r] = jnp.sum(jnp.where(lane_of[0:1] == mine, residual, 0.0))
    out_copy.wait()


def solution(mesh):
    n_band, n_grid = mesh.shape["band"], mesh.shape["grid"]

    def on_device(trial_bands, potential):
        nb, nz, nx, ny = trial_bands.shape
        rows = nz * nx
        bands = nb * n_band
        share = 8 * -(-rows // (8 * n_band))
        width = 128 * -(-3 * bands // 128)
        cells = rows * n_grid * ny
        sizes = (nb, nz, nx, n_band, n_grid, share, width, cells)
        f32 = jnp.float32

        def field(halo):
            return pltpu.VMEM((nb, rows + 2 * halo * nx, ny), f32)

        filtered, projected, residual = pl.pallas_call(
            functools.partial(kernel, sizes),
            out_shape=(
                jax.ShapeDtypeStruct((nb, rows, ny), f32),
                jax.ShapeDtypeStruct((nb, bands), f32),
                jax.ShapeDtypeStruct((nb,), f32),
            ),
            in_specs=[pl.BlockSpec(memory_space=pl.ANY)] * 2,
            out_specs=(
                pl.BlockSpec(memory_space=pl.ANY),
                pl.BlockSpec(memory_space=pltpu.VMEM),
                pl.BlockSpec(memory_space=pltpu.SMEM),
            ),
            scratch_shapes=[
                field(4),
                pltpu.VMEM((rows + 4 * nx, ny), f32),
                field(2),
                field(4),
                field(2),
                field(2),
                pltpu.VMEM((nb, share * n_band, ny), f32),
                pltpu.VMEM((nb, share * n_band, ny), f32),
                pltpu.VMEM((n_band, nb, share, ny), f32),
                pltpu.VMEM((n_band, nb, share, ny), f32),
                pltpu.VMEM((n_band, bands + 8, width), f32),
                pltpu.VMEM((n_grid, bands + 8, width), f32),
                pltpu.SemaphoreType.DMA((8,)),
                pltpu.SemaphoreType.DMA((8,)),
            ]
            + [pltpu.SemaphoreType.DMA((n_band,))] * 6
            + [pltpu.SemaphoreType.DMA((n_grid,))] * 2
            + [pltpu.SemaphoreType.DMA((3,))],
            compiler_params=pltpu.CompilerParams(
                collective_id=0, has_side_effects=True, vmem_limit_bytes=48 * 1024 * 1024
            ),
        )(trial_bands.reshape(nb, rows, ny), potential.reshape(rows, ny))
        return filtered.reshape(nb, nz, nx, ny), projected, residual

    return jax.shard_map(
        on_device,
        mesh=mesh,
        in_specs=(P("band", "grid", None, None), P("grid", None, None)),
        out_specs=(P("band", "grid", None, None), P("band", None), P("band")),
        check_vma=False,
    )
```

time: 108 us -> 49.1 us (0.45)
  Pallas kernels: 0 us -> 44.6 us
  blocking collectives: 38.4 us -> 0 us
  waiting for transfers between devices: 20.3 us -> 0 us
  starting transfers between devices: 19.4 us -> 0 us
  local copies, waits for them, and re-layouts: 17.5 us -> 3.68 us
  other arithmetic: 9.13 us -> 0 us
  matrix products: 1.5 us -> 0 us
    pallas_call x0 -> x1, Pallas kernels: none -> 44.6 us  [on_device(): pl.pallas_call(functools.partial(kernel, sizes), out_shape=(jax.ShapeDtyp...]
    psum x1 -> x0, blocking collectives: 38.4 us -> none  [on_device(): lax.psum((margin_part, image_part, norm_full), ('band', 'grid'))]
    all_to_all x2 -> x0, waiting for transfers between devices: 11.8 us -> none  [the longest x1 9.35 us: on_device(): lax.all_to_all(flat_image, 'band', split_axis=1, concat_axis=0, tiled=True)]
    ppermute x10 -> x0, starting transfers between devices: 10.4 us -> none  [the longest x5 7.26 us: padded_2(): lax.ppermute(tail, axis, [(i, (i + 1) % count) for i in range(count)])]
    all_to_all x2 -> x0, starting transfers between devices: 9.05 us -> none  [the longest x1 5.1 us: on_device(): lax.all_to_all(flat_bands, 'band', split_axis=1, concat_axis=0, tiled=True)]
    ppermute x10 -> x0, waiting for transfers between devices: 8.53 us -> none  [the longest x5 7.58 us: padded_2(): lax.ppermute(tail, axis, [(i, (i + 1) % count) for i in range(count)])]
    slice x45 -> x0, local copies, waits for them, and re-layouts: 8.09 us -> none  [the longest x10 4.15 us: operate(): far_sum = far_sum + jnp.roll(field_in, 2, 3) + jnp.roll(field_in, -2, 3)]
    all_to_all x6 -> x0, local copies, waits for them, and re-layouts: 6.16 us -> none  [the longest x3 3.91 us: on_device(): lax.all_to_all(flat_bands, 'band', split_axis=1, concat_axis=0, tiled=True)]
  transfers between devices with their start and end apart: 12 -> 0, of which waited for: 9 -> 0; matrix products, arithmetic and copies ran while one was open for 6% -> 0% of each run, Pallas kernels for 0% -> 0%
where the time goes in v1:
time: 49.1 us; the launch traced here: 48.9 us
  Pallas kernels  44.6 us (91%)
  local copies, waits for them, and re-layouts  3.68 us (7%)
  between operations  0.65 us (1%)
    pallas_call x1, Pallas kernels, on_device(): pl.pallas_call(functools.partial(kernel, sizes), out_shape=(jax.ShapeDtyp...  44.6 us
    unnamed x7, local copies, waits for them, and re-layouts  3.68 us

profile of v1, /device:TPU:0, one launch (start us, length us, event | category | flops | bytes accessed | tf_op | source)
XLA Modules:
  0.0 48.9 jit_solution(16507696723408392919)
XLA Ops:
  0.6 0.0 copy-start
  0.6 1.0 %copy-done = f32[2,10,32,128]{3,2,1,0:T(8,128)S(1)} copy-done((f32[2,10,32,128]{3,2,1,0:T(8,128)S(1)}, f32[2,10,32,128]{3,2,1,0:T(8,128)}, u32[]{:S(2)}) %copy-start) | copy-done | bytes 327704
  1.6 0.0 copy-start.1
  1.6 0.9 %copy-done.1 = f32[10,32,128]{2,1,0:T(8,128)S(1)} copy-done((f32[10,32,128]{2,1,0:T(8,128)S(1)}, f32[10,32,128]{2,1,0:T(8,128)}, u32[]{:S(2)}) %copy-start.1) | copy-done | bytes 163864
  2.5 44.6 %shard_map.49 = (f32[2,320,128]{2,1,0:T(8,128)S(1)}, f32[2,16]{1,0:T(2,128)S(1)}, f32[2]{0:T(128)S(1)}) custom-call(f32[2,320,128]{2,1,0:T(8,128)S(1)} %bitcast.4, f32[320,128]{1,0:T(8,128)S(1)} %bitcast.5), custom_call_target="tpu_custom_call" | custom-call | tf_op jit(solution)/shard_map/pallas_call | solution.py:363
  47.1 0.7 %copy.8 = f32[2,10,32,128]{3,2,1,0:T(8,128)} copy(f32[2,10,32,128]{3,2,1,0:T(8,128)S(1)} %bitcast.3) | data formatting | bytes 655360
  47.8 0.6 %copy.9 = f32[2,16]{1,0:T(2,128)} copy(f32[2,16]{1,0:T(2,128)S(1)} %get-tuple-element.13) | data formatting | bytes 256
  48.4 0.5 %copy.10 = f32[2]{0:T(128)} copy(f32[2]{0:T(128)S(1)} %get-tuple-element.14) | data formatting | bytes 16
Async XLA Ops:
  0.6 1.0 %copy-start = (f32[2,10,32,128]{3,2,1,0:T(8,128)S(1)}, f32[2,10,32,128]{3,2,1,0:T(8,128)}, u32[]{:S(2)}) copy-start(f32[2,10,32,128]{3,2,1,0:T(8,128)} %param.2) | copy-start | bytes 983044
  1.6 0.9 %copy-start.1 = (f32[10,32,128]{2,1,0:T(8,128)S(1)}, f32[10,32,128]{2,1,0:T(8,128)}, u32[]{:S(2)}) copy-start(f32[10,32,128]{2,1,0:T(8,128)} %param.3) | copy-start | bytes 491524

commit v2 on v1

v2 whole, which is shorter than its diff:
```python
import functools

import jax
import jax.numpy as jnp
from jax import lax
from jax.experimental import pallas as pl
from jax.experimental.pallas import tpu as pltpu
from jax.sharding import PartitionSpec as P

CENTER = 4.25
HALF_WIDTH = 3.75
LOWEST = -2.0
SIGMA_ONE = HALF_WIDTH / (LOWEST - CENTER)
MESH = pl.DeviceIdType.MESH
VMEM_LIMIT = 64 * 1024 * 1024
HIGHEST = lax.Precision.HIGHEST
CONTRACT_LANES = (((1,), (1,)), ((), ()))


def filter_steps():
    sigma_now = SIGMA_ONE
    steps = [(SIGMA_ONE / HALF_WIDTH, 0.0)]
    for _ in range(3):
        sigma_next = 1.0 / (2.0 / SIGMA_ONE - sigma_now)
        steps.append((2.0 * sigma_next / HALF_WIDTH, sigma_now * sigma_next))
        sigma_now = sigma_next
    return steps


def kernel(
    sizes,
    x_hbm,
    v_hbm,
    f_out,
    total_out,
    x0,
    vp,
    y1,
    y2,
    y3,
    y4,
    image,
    f_share,
    f_all,
    h_all,
    part_a,
    part_b,
    halo_send,
    halo_recv,
    f_send,
    f_recv,
    h_send,
    h_recv,
    a_send,
    a_recv,
    b_send,
    b_recv,
    local_sem,
):
    nb, nz, nx, n_band, n_grid, share, width = sizes
    rows = nz * nx
    bands = nb * n_band
    me = lax.axis_index("band")
    slab = lax.axis_index("grid")
    right = lax.rem(slab + 1, n_grid)
    left = lax.rem(slab + n_grid - 1, n_grid)
    ny = x0.shape[-1]

    own = [
        pltpu.make_async_copy(x_hbm, x0.at[:, pl.ds(4 * nx, rows)], local_sem.at[0]),
        pltpu.make_async_copy(v_hbm, vp.at[pl.ds(2 * nx, rows)], local_sem.at[1]),
    ]
    for copy in own:
        copy.start()

    barrier = pltpu.get_barrier_semaphore()

    def greet_band(d, carry):
        pl.semaphore_signal(
            barrier, inc=1, device_id=(lax.rem(me + d, n_band), slab), device_id_type=MESH
        )
        return carry

    def greet_grid(d, carry):
        pl.semaphore_signal(
            barrier, inc=1, device_id=(me, lax.rem(slab + d, n_grid)), device_id_type=MESH
        )
        return carry

    lax.fori_loop(1, n_grid, greet_grid, 0)
    lax.fori_loop(1, n_band, greet_band, 0)
    pl.semaphore_wait(barrier, n_band + n_grid - 2)

    def halo_copy(index, src, dst, to):
        return pltpu.make_async_remote_copy(
            src_ref=src,
            dst_ref=dst,
            send_sem=halo_send.at[index],
            recv_sem=halo_recv.at[index],
            device_id=(me, to),
            device_id_type=MESH,
        )

    def up(index, band, src, first, dst, depth):
        return halo_copy(
            2 * (nb * index + band),
            src.at[band, pl.ds((first + nz - depth) * nx, depth * nx)],
            dst.at[band, pl.ds(0, depth * nx)],
            right,
        )

    def down(index, band, src, first, dst, depth):
        return halo_copy(
            2 * (nb * index + band) + 1,
            src.at[band, pl.ds(first * nx, depth * nx)],
            dst.at[band, pl.ds((nz + depth) * nx, depth * nx)],
            left,
        )

    def swap(index, band, src, first, dst, depth):
        return [up(index, band, src, first, dst, depth), down(index, band, src, first, dst, depth)]

    swap_x = [swap(0, band, x_hbm, 0, x0, 4) for band in range(nb)]
    swap_2 = [swap(1, band, y2, 4, y2, 4) for band in range(nb)]
    swap_4 = [swap(2, band, y4, 2, y4, 2) for band in range(nb)]
    swap_v = [
        halo_copy(6 * nb, v_hbm.at[pl.ds((nz - 2) * nx, 2 * nx)], vp.at[pl.ds(0, 2 * nx)], right),
        halo_copy(6 * nb + 1, v_hbm.at[pl.ds(0, 2 * nx)], vp.at[pl.ds((nz + 2) * nx, 2 * nx)], left),
    ]
    for copy in swap_x[0] + swap_v + [copy for band in range(1, nb) for copy in swap_x[band]]:
        copy.start()

    steps = filter_steps()

    def planes(band, lo, hi, src, src_halo, dsts, scale, center, prev=None, prev_halo=0, weight=0.0):
        def at(ref, halo, plane):
            return ref[band, pl.ds(pl.multiple_of((plane + halo) * nx, nx), nx), :]

        def body(step, carry):
            plane = lo + step
            local = vp[pl.ds(pl.multiple_of((plane + 2) * nx, nx), nx), :]
            local = (local + (3.75 - center)) * scale
            here = at(src, src_halo, plane)
            near = at(src, src_halo, plane - 1) + at(src, src_halo, plane + 1)
            far = at(src, src_halo, plane - 2) + at(src, src_halo, plane + 2)
            near += pltpu.roll(here, 1, 0) + pltpu.roll(here, nx - 1, 0)
            far += pltpu.roll(here, 2, 0) + pltpu.roll(here, nx - 2, 0)
            near += pltpu.roll(here, 1, 1) + pltpu.roll(here, ny - 1, 1)
            far += pltpu.roll(here, 2, 1) + pltpu.roll(here, ny - 2, 1)
            value = local * here - near * (scale * 2.0 / 3.0) + far * (scale / 24.0)
            if prev is not None:
                value = value - weight * at(prev, prev_halo, plane)
            for dst, halo in dsts:
                dst[band, pl.ds(pl.multiple_of((plane + halo) * nx, nx), nx), :] = value
            return carry

        lax.fori_loop(0, hi - lo, body, 0, unroll=hi - lo)

    step_1 = functools.partial(planes, src=x0, src_halo=4, dsts=[(y1, 2)], scale=steps[0][0], center=CENTER)
    step_2 = functools.partial(
        planes, src=y1, src_halo=2, dsts=[(y2, 4)], scale=steps[1][0], center=CENTER,
        prev=x0, prev_halo=4, weight=steps[1][1],
    )
    step_3 = functools.partial(
        planes, src=y2, src_halo=4, dsts=[(y3, 2)], scale=steps[2][0], center=CENTER,
        prev=y1, prev_halo=2, weight=steps[2][1],
    )
    step_4 = functools.partial(
        planes, src=y3, src_halo=2, dsts=[(y4, 2), (f_share, 0)], scale=steps[3][0], center=CENTER,
        prev=y2, prev_halo=4, weight=steps[3][1],
    )
    last = functools.partial(planes, src=y4, src_halo=2, dsts=[(image, 0)], scale=1.0, center=0.0)

    padded = share * n_band
    if padded != rows:
        f_share[:, rows:, :] = jnp.zeros((nb, padded - rows, ny), jnp.float32)
        image[:, rows:, :] = jnp.zeros((nb, padded - rows, ny), jnp.float32)

    def to_band(band, src, dst, send, recv, d):
        partner = lax.rem(me + d, n_band)
        return pltpu.make_async_remote_copy(
            src_ref=src.at[band, pl.ds(pl.multiple_of(partner * share, 8), share)],
            dst_ref=dst.at[me, band],
            send_sem=send.at[band, d],
            recv_sem=recv.at[band, n_band - d],
            device_id=(partner, slab),
            device_id_type=MESH,
        )

    def start_band(band, *args):
        def body(d, carry):
            to_band(band, *args, d).start()
            return carry

        lax.fori_loop(1, n_band, body, 0)

    def wait_band(band, *args):
        def body(d, carry):
            to_band(band, *args, d).wait()
            return carry

        lax.fori_loop(1, n_band, body, 0)

    f_route = (f_share, f_all, f_send, f_recv)
    h_route = (image, h_all, h_send, h_recv)

    for copy in own:
        copy.wait()
    for band in range(nb):
        step_1(band, 2, nz - 2)
    for band in range(nb):
        for copy in swap_x[band] + (swap_v if band == 0 else []):
            copy.wait()
        step_1(band, -2, 2)
        step_1(band, nz - 2, nz + 2)
        step_2(band, 0, 4)
        swap_2[band][1].start()
        step_2(band, nz - 4, nz)
        swap_2[band][0].start()
        step_2(band, 4, nz - 4)
    for band in range(nb):
        step_3(band, 2, nz - 2)
        for copy in swap_2[band]:
            copy.wait()
        step_3(band, -2, 2)
        step_3(band, nz - 2, nz + 2)
        step_4(band, 0, 2)
        swap_4[band][1].start()
        step_4(band, nz - 2, nz)
        swap_4[band][0].start()
        step_4(band, 2, nz - 2)
        start_band(band, *f_route)
    out_copy = pltpu.make_async_copy(f_share.at[:, pl.ds(0, rows)], f_out, local_sem.at[2])
    out_copy.start()
    for band in range(nb):
        last(band, 2, nz - 2)
        for copy in swap_4[band]:
            copy.wait()
        last(band, 0, 2)
        last(band, nz - 2, nz)
        start_band(band, *h_route)

    own_rows = pl.ds(pl.multiple_of(me * share, 8), share)
    f_all[me] = f_share[:, own_rows, :]
    h_all[me] = image[:, own_rows, :]

    def on_lanes(ref):
        whole = ref[...]
        tiles = [
            whole[:, :, 8 * t : 8 * t + 8, :].reshape(bands * 8, ny) for t in range(share // 8)
        ]
        return jnp.concatenate(tiles, axis=1)

    stretched = bands * 8
    same = (
        lax.broadcasted_iota(jnp.int32, (stretched, stretched), 0) % 8
        == lax.broadcasted_iota(jnp.int32, (stretched, stretched), 1) % 8
    )
    column = lax.broadcasted_iota(jnp.int32, (stretched, width), 0) // 8
    lane = lax.broadcasted_iota(jnp.int32, (stretched, width), 1)

    def folded(gram, offset):
        gram = jnp.where(same, gram, 0.0).reshape(bands, 8, stretched).sum(axis=1)
        pick = jnp.where(column + offset == lane, 1.0, 0.0)
        return jnp.dot(gram, pick, precision=HIGHEST, preferred_element_type=jnp.float32)

    for band in range(nb):
        wait_band(band, *f_route)
    filtered = on_lanes(f_all)
    margin = lax.dot_general(
        filtered, filtered, CONTRACT_LANES, precision=HIGHEST, preferred_element_type=jnp.float32
    )
    top = folded(margin, 0)
    for band in range(nb):
        wait_band(band, *h_route)
    images = on_lanes(h_all)
    mixed = lax.dot_general(
        filtered, images, CONTRACT_LANES, precision=HIGHEST, preferred_element_type=jnp.float32
    )
    top = top + folded(mixed, bands)
    whole = h_all[...]
    squares = (whole * whole).sum(axis=2).reshape(bands, ny)
    norm_lane = lax.broadcasted_iota(jnp.int32, (bands, width), 1) - 2 * bands * (bands // 8)
    norm_row = lax.broadcasted_iota(jnp.int32, (bands, width), 0)
    norms = jnp.sum(squares, axis=1, keepdims=True)
    norms = jnp.sum(jnp.where(norm_lane == norm_row, norms, 0.0), axis=0, keepdims=True)
    packed = top[0:8]
    for group in range(1, bands // 8):
        packed = packed + pltpu.roll(top[8 * group : 8 * group + 8], 2 * bands * group, 1)
    part_a[me] = packed + norms

    def sum_over(part, count, here, target, send, recv):
        def copy(d):
            return pltpu.make_async_remote_copy(
                src_ref=part.at[here],
                dst_ref=part.at[here],
                send_sem=send.at[d],
                recv_sem=recv.at[count - d],
                device_id=target(lax.rem(here + d, count)),
                device_id_type=MESH,
            )

        def start(d, carry):
            copy(d).start()
            return carry

        def wait(d, carry):
            copy(d).wait()
            return carry

        lax.fori_loop(1, count, start, 0)
        lax.fori_loop(1, count, wait, 0)
        return jnp.sum(part[...], axis=0)

    part_b[slab] = sum_over(part_a, n_band, me, lambda j: (j, slab), a_send, a_recv)
    total_out[...] = sum_over(part_b, n_grid, slab, lambda j: (me, j), b_send, b_recv)
    out_copy.wait()


def small_kernel(sizes, f_in, total_in, f_out, projected_out, residual_out, out_sem):
    nb, bands, width, cells = sizes
    out_copy = pltpu.make_async_copy(f_in, f_out, out_sem)
    out_copy.start()
    me = lax.axis_index("band")
    total = total_in[...] * (1.0 / cells)
    groups = [total] + [
        pltpu.roll(total, width - 2 * bands * group, 1) for group in range(1, bands // 8 + 1)
    ]
    row_of = lax.broadcasted_iota(jnp.int32, (bands, width), 0)
    lane_of = lax.broadcasted_iota(jnp.int32, (bands, width), 1)
    work = jnp.concatenate(groups[:-1], axis=0)
    unit = jnp.where(lane_of == row_of + 2 * bands, 1.0, 0.0)
    work = jnp.where(lane_of < 2 * bands, work, unit)
    for k in range(bands):
        pivot = work[k : k + 1, k : k + 1]
        inverse = lax.rsqrt(pivot)
        inverse = inverse * (1.5 - 0.5 * pivot * inverse * inverse)
        row = work[k : k + 1, :] * inverse
        factor_column = work[:, k : k + 1] * inverse
        below = work - factor_column * row
        work = jnp.where(row_of > k, below, jnp.where(row_of == k, row, work))
    coefficients = jnp.where(lane_of < bands, pltpu.roll(work, width - bands, 1), 0.0)
    inverse_factor = jnp.where(lane_of < bands, pltpu.roll(work, width - 2 * bands, 1), 0.0)
    projected = lax.dot_general(
        inverse_factor,
        coefficients,
        CONTRACT_LANES,
        precision=HIGHEST,
        preferred_element_type=jnp.float32,
    )
    residual = groups[-1][0:1] - jnp.sum(coefficients * coefficients, axis=0, keepdims=True)
    square_rows = lax.broadcasted_iota(jnp.int32, (bands, bands), 0)
    for r in range(nb):
        mine = me * nb + r
        projected_out[r : r + 1, :] = jnp.sum(
            jnp.where(square_rows == mine, projected, 0.0), axis=0, keepdims=True
        )
        residual_out[r] = jnp.sum(jnp.where(lane_of[0:1] == mine, residual, 0.0))
    out_copy.wait()


def solution(mesh):
    n_band, n_grid = mesh.shape["band"], mesh.shape["grid"]

    def on_device(trial_bands, potential):
        nb, nz, nx, ny = trial_bands.shape
        rows = nz * nx
        bands = nb * n_band
        share = 8 * -(-rows // (8 * n_band))
        width = 128 * -(-(2 * bands * (bands // 8) + bands) // 128)
        cells = rows * n_grid * ny
        f32 = jnp.float32

        def field(halo):
            return pltpu.VMEM((nb, rows + 2 * halo * nx, ny), f32)

        shares, total = pl.pallas_call(
            functools.partial(kernel, (nb, nz, nx, n_band, n_grid, share, width)),
            out_shape=(
                jax.ShapeDtypeStruct((nb, rows, ny), f32),
                jax.ShapeDtypeStruct((8, width), f32),
            ),
            in_specs=[pl.BlockSpec(memory_space=pltpu.HBM)] * 2,
            out_specs=(
                pl.BlockSpec(memory_space=pltpu.HBM),
                pl.BlockSpec(memory_space=pltpu.VMEM),
            ),
            scratch_shapes=[
                field(4),
                pltpu.VMEM((rows + 4 * nx, ny), f32),
                field(2),
                field(4),
                field(2),
                field(2),
                pltpu.VMEM((nb, share * n_band, ny), f32),
                pltpu.VMEM((nb, share * n_band, ny), f32),
                pltpu.VMEM((n_band, nb, share, ny), f32),
                pltpu.VMEM((n_band, nb, share, ny), f32),
                pltpu.VMEM((n_band, 8, width), f32),
                pltpu.VMEM((n_grid, 8, width), f32),
                pltpu.SemaphoreType.DMA((6 * nb + 2,)),
                pltpu.SemaphoreType.DMA((6 * nb + 2,)),
            ]
            + [pltpu.SemaphoreType.DMA((nb, n_band))] * 4
            + [pltpu.SemaphoreType.DMA((n_band,))] * 2
            + [pltpu.SemaphoreType.DMA((n_grid,))] * 2
            + [pltpu.SemaphoreType.DMA((3,))],
            compiler_params=pltpu.CompilerParams(
                collective_id=0, has_side_effects=True, vmem_limit_bytes=VMEM_LIMIT
            ),
        )(trial_bands.reshape(nb, rows, ny), potential.reshape(rows, ny))
        filtered, projected, residual = pl.pallas_call(
            functools.partial(small_kernel, (nb, bands, width, cells)),
            out_shape=(
                jax.ShapeDtypeStruct((nb, rows, ny), f32),
                jax.ShapeDtypeStruct((nb, bands), f32),
                jax.ShapeDtypeStruct((nb,), f32),
            ),
            in_specs=[
                pl.BlockSpec(memory_space=pl.ANY),
                pl.BlockSpec(memory_space=pltpu.VMEM),
            ],
            out_specs=(
                pl.BlockSpec(memory_space=pltpu.HBM),
                pl.BlockSpec(memory_space=pltpu.VMEM),
                pl.BlockSpec(memory_space=pltpu.SMEM),
            ),
            scratch_shapes=[pltpu.SemaphoreType.DMA],
            compiler_params=pltpu.CompilerParams(vmem_limit_bytes=VMEM_LIMIT),
        )(shares, total)
        return filtered.reshape(nb, nz, nx, ny), projected, residual

    return jax.shard_map(
        on_device,
        mesh=mesh,
        in_specs=(P("band", "grid", None, None), P("grid", None, None)),
        out_specs=(P("band", "grid", None, None), P("band", None), P("band")),
        check_vma=False,
    )
```

time: 49.1 us -> 52.4 us (1.067)
  Pallas kernels: 44.6 us -> 51.6 us
  local copies, waits for them, and re-layouts: 3.68 us -> 0 us
    pallas_call x1 -> x2, Pallas kernels: 44.6 us -> 51.6 us  [the longest x1 39.3 us: on_device(): pl.pallas_call(functools.partial(kernel, (nb, nz, nx, n_band, n_grid, sha...]
    unnamed x7 -> x0, local copies, waits for them, and re-layouts: 3.68 us -> none
where the time goes in v2:
time: 52.4 us; the launch traced here: 52.2 us
  Pallas kernels  51.6 us (98%)
  between operations  0.64 us (1%)
    pallas_call x1, Pallas kernels, on_device(): pl.pallas_call(functools.partial(kernel, (nb, nz, nx, n_band, n_grid, sha...  39.3 us
    pallas_call x1, Pallas kernels, on_device(): pl.pallas_call(functools.partial(small_kernel, (nb, bands, width, cells))...  12.3 us

profile of v2, /device:TPU:0, one launch (start us, length us, event | category | flops | bytes accessed | tf_op | source)
XLA Modules:
  0.0 52.2 jit_solution(16233981471690464985)
XLA Ops:
  0.6 39.3 %shard_map.49 = (f32[2,320,128]{2,1,0:T(8,128)}, f32[8,128]{1,0:T(8,128)}) custom-call(f32[2,320,128]{2,1,0:T(8,128)} %bitcast.3, f32[320,128]{1,0:T(8,128)} %bitcast.4), custom_call_target="tpu_custom_call" | custom-call | tf_op jit(solution)/shard_map/pallas_call | solution.py:377
  39.9 12.3 %shard_map.50 = (f32[2,320,128]{2,1,0:T(8,128)}, f32[2,16]{1,0:T(2,128)}, f32[2]{0:T(128)}) custom-call(f32[2,320,128]{2,1,0:T(8,128)} %get-tuple-element.8.f_in, f32[8,128]{1,0:T(8,128)} %get-tuple-element.9.total_in), custom_call_target="tpu_custom_call" | custom-call | tf_op jit(solution)/shard_map/pallas_call | solution.py:412

commit v3 on v2

--- a/solution.py
+++ b/solution.py
@@ -32,7 +32,8 @@
     x_hbm,
     v_hbm,
     f_out,
-    total_out,
+    projected_out,
+    residual_out,
     x0,
     vp,
     y1,
@@ -57,7 +58,7 @@
     b_recv,
     local_sem,
 ):
-    nb, nz, nx, n_band, n_grid, share, width = sizes
+    nb, nz, nx, n_band, n_grid, share, width, cells = sizes
     rows = nz * nx
     bands = nb * n_band
     me = lax.axis_index("band")
@@ -120,41 +121,68 @@
     def swap(index, band, src, first, dst, depth):
         return [up(index, band, src, first, dst, depth), down(index, band, src, first, dst, depth)]
 
-    swap_x = [swap(0, band, x_hbm, 0, x0, 4) for band in range(nb)]
-    swap_2 = [swap(1, band, y2, 4, y2, 4) for band in range(nb)]
-    swap_4 = [swap(2, band, y4, 2, y4, 2) for band in range(nb)]
+    def swap_x(band):
+        return swap(0, band, x_hbm, 0, x0, 4)
+
+    def swap_2(band):
+        return swap(1, band, y2, 4, y2, 4)
+
+    def swap_4(band):
+        return swap(2, band, y4, 2, y4, 2)
+
+    def each_band(body):
+        def step(band, carry):
+            body(band)
+            return carry
+
+        lax.fori_loop(0, nb, step, 0)
+
     swap_v = [
         halo_copy(6 * nb, v_hbm.at[pl.ds((nz - 2) * nx, 2 * nx)], vp.at[pl.ds(0, 2 * nx)], right),
         halo_copy(6 * nb + 1, v_hbm.at[pl.ds(0, 2 * nx)], vp.at[pl.ds((nz + 2) * nx, 2 * nx)], left),
     ]
-    for copy in swap_x[0] + swap_v + [copy for band in range(1, nb) for copy in swap_x[band]]:
-        copy.start()
+
+    def start_all(copies):
+        for copy in copies:
+            copy.start()
+
+    def wait_all(copies):
+        for copy in copies:
+            copy.wait()
+
+    start_all(swap_v)
+    each_band(lambda band: start_all(swap_x(band)))
 
     steps = filter_steps()
 
-    def planes(band, lo, hi, src, src_halo, dsts, scale, center, prev=None, prev_halo=0, weight=0.0):
+    def planes(band, pieces, src, src_halo, dsts, scale, center, prev=None, prev_halo=0, weight=0.0):
+        lo, hi = pieces[0]
+        pairs = (hi - lo) // 2
+        jump = pieces[-1][0] - hi
+
         def at(ref, halo, plane):
             return ref[band, pl.ds(pl.multiple_of((plane + halo) * nx, nx), nx), :]
 
         def body(step, carry):
-            plane = lo + step
-            local = vp[pl.ds(pl.multiple_of((plane + 2) * nx, nx), nx), :]
-            local = (local + (3.75 - center)) * scale
-            here = at(src, src_halo, plane)
-            near = at(src, src_halo, plane - 1) + at(src, src_halo, plane + 1)
-            far = at(src, src_halo, plane - 2) + at(src, src_halo, plane + 2)
-            near += pltpu.roll(here, 1, 0) + pltpu.roll(here, nx - 1, 0)
-            far += pltpu.roll(here, 2, 0) + pltpu.roll(here, nx - 2, 0)
-            near += pltpu.roll(here, 1, 1) + pltpu.roll(here, ny - 1, 1)
-            far += pltpu.roll(here, 2, 1) + pltpu.roll(here, ny - 2, 1)
-            value = local * here - near * (scale * 2.0 / 3.0) + far * (scale / 24.0)
-            if prev is not None:
-                value = value - weight * at(prev, prev_halo, plane)
-            for dst, halo in dsts:
-                dst[band, pl.ds(pl.multiple_of((plane + halo) * nx, nx), nx), :] = value
-            return carry
-
-        lax.fori_loop(0, hi - lo, body, 0, unroll=hi - lo)
+            first = lo + 2 * step + (step // pairs) * jump
+            for plane in (first, first + 1):
+                local = vp[pl.ds(pl.multiple_of((plane + 2) * nx, nx), nx), :]
+                local = (local + (3.75 - center)) * scale
+                here = at(src, src_halo, plane)
+                near = at(src, src_halo, plane - 1) + at(src, src_halo, plane + 1)
+                far = at(src, src_halo, plane - 2) + at(src, src_halo, plane + 2)
+                near += pltpu.roll(here, 1, 0) + pltpu.roll(here, nx - 1, 0)
+                far += pltpu.roll(here, 2, 0) + pltpu.roll(here, nx - 2, 0)
+                near += pltpu.roll(here, 1, 1) + pltpu.roll(here, ny - 1, 1)
+                far += pltpu.roll(here, 2, 1) + pltpu.roll(here, ny - 2, 1)
+                value = local * here - near * (scale * 2.0 / 3.0) + far * (scale / 24.0)
+                if prev is not None:
+                    value = value - weight * at(prev, prev_halo, plane)
+                for dst, halo in dsts:
+                    dst[band, pl.ds(pl.multiple_of((plane + halo) * nx, nx), nx), :] = value
+            return carry
+
+        lax.fori_loop(0, pairs * len(pieces), body, 0)
 
     step_1 = functools.partial(planes, src=x0, src_halo=4, dsts=[(y1, 2)], scale=steps[0][0], center=CENTER)
     step_2 = functools.partial(
@@ -204,80 +232,79 @@
     f_route = (f_share, f_all, f_send, f_recv)
     h_route = (image, h_all, h_send, h_recv)
 
-    for copy in own:
-        copy.wait()
-    for band in range(nb):
-        step_1(band, 2, nz - 2)
-    for band in range(nb):
-        for copy in swap_x[band] + (swap_v if band == 0 else []):
-            copy.wait()
-        step_1(band, -2, 2)
-        step_1(band, nz - 2, nz + 2)
-        step_2(band, 0, 4)
-        swap_2[band][1].start()
-        step_2(band, nz - 4, nz)
-        swap_2[band][0].start()
-        step_2(band, 4, nz - 4)
-    for band in range(nb):
-        step_3(band, 2, nz - 2)
-        for copy in swap_2[band]:
-            copy.wait()
-        step_3(band, -2, 2)
-        step_3(band, nz - 2, nz + 2)
-        step_4(band, 0, 2)
-        swap_4[band][1].start()
-        step_4(band, nz - 2, nz)
-        swap_4[band][0].start()
-        step_4(band, 2, nz - 2)
+    inner = [(2, nz - 2)]
+    rim = [(0, 2), (nz - 2, nz)]
+    halo_rim = [(-2, 2), (nz - 2, nz + 2)]
+
+    def to_y2(band):
+        wait_all(swap_x(band))
+        step_1(band, halo_rim)
+        step_2(band, [(0, 4), (nz - 4, nz)])
+        start_all(swap_2(band))
+        if nz > 8:
+            step_2(band, [(4, nz - 4)])
+
+    def to_y4(band):
+        step_3(band, inner)
+        wait_all(swap_2(band))
+        step_3(band, halo_rim)
+        step_4(band, rim)
+        start_all(swap_4(band))
+        step_4(band, inner)
         start_band(band, *f_route)
+
+    def to_image(band):
+        last(band, inner)
+        wait_all(swap_4(band))
+        last(band, rim)
+        start_band(band, *h_route)
+
+    wait_all(own)
+    each_band(lambda band: step_1(band, inner))
+    wait_all(swap_v)
+    each_band(to_y2)
+    each_band(to_y4)
     out_copy = pltpu.make_async_copy(f_share.at[:, pl.ds(0, rows)], f_out, local_sem.at[2])
     out_copy.start()
-    for band in range(nb):
-        last(band, 2, nz - 2)
-        for copy in swap_4[band]:
-            copy.wait()
-        last(band, 0, 2)
-        last(band, nz - 2, nz)
-        start_band(band, *h_route)
+    each_band(to_image)
 
     own_rows = pl.ds(pl.multiple_of(me * share, 8), share)
     f_all[me] = f_share[:, own_rows, :]
     h_all[me] = image[:, own_rows, :]
-
-    def on_lanes(ref):
-        whole = ref[...]
-        tiles = [
-            whole[:, :, 8 * t : 8 * t + 8, :].reshape(bands * 8, ny) for t in range(share // 8)
-        ]
-        return jnp.concatenate(tiles, axis=1)
 
     stretched = bands * 8
     same = (
         lax.broadcasted_iota(jnp.int32, (stretched, stretched), 0) % 8
         == lax.broadcasted_iota(jnp.int32, (stretched, stretched), 1) % 8
     )
+
+    def gram(ref):
+        def tile(of, t):
+            return of[:, :, pl.ds(pl.multiple_of(8 * t, 8), 8), :].reshape(stretched, ny)
+
+        def body(t, total):
+            return total + lax.dot_general(
+                tile(f_all, t),
+                tile(ref, t),
+                CONTRACT_LANES,
+                precision=HIGHEST,
+                preferred_element_type=jnp.float32,
+            )
+
+        return lax.fori_loop(0, share // 8, body, jnp.zeros((stretched, stretched), jnp.float32))
+
     column = lax.broadcasted_iota(jnp.int32, (stretched, width), 0) // 8
     lane = lax.broadcasted_iota(jnp.int32, (stretched, width), 1)
 
-    def folded(gram, offset):
-        gram = jnp.where(same, gram, 0.0).reshape(bands, 8, stretched).sum(axis=1)
+    def folded(products, offset):
+        products = jnp.where(same, products, 0.0).reshape(bands, 8, stretched).sum(axis=1)
         pick = jnp.where(column + offset == lane, 1.0, 0.0)
-        return jnp.dot(gram, pick, precision=HIGHEST, preferred_element_type=jnp.float32)
-
-    for band in range(nb):
-        wait_band(band, *f_route)
-    filtered = on_lanes(f_all)
-    margin = lax.dot_general(
-        filtered, filtered, CONTRACT_LANES, precision=HIGHEST, preferred_element_type=jnp.float32
-    )
-    top = folded(margin, 0)
-    for band in range(nb):
-        wait_band(band, *h_route)
-    images = on_lanes(h_all)
-    mixed = lax.dot_general(
-        filtered, images, CONTRACT_LANES, precision=HIGHEST, preferred_element_type=jnp.float32
-    )
-    top = top + folded(mixed, bands)
+        return jnp.dot(products, pick, precision=HIGHEST, preferred_element_type=jnp.float32)
+
+    each_band(lambda band: wait_band(band, *f_route))
+    top = folded(gram(f_all), 0)
+    each_band(lambda band: wait_band(band, *h_route))
+    top = top + folded(gram(h_all), bands)
     whole = h_all[...]
     squares = (whole * whole).sum(axis=2).reshape(bands, ny)
     norm_lane = lax.broadcasted_iota(jnp.int32, (bands, width), 1) - 2 * bands * (bands // 8)
@@ -313,16 +340,7 @@
         return jnp.sum(part[...], axis=0)
 
     part_b[slab] = sum_over(part_a, n_band, me, lambda j: (j, slab), a_send, a_recv)
-    total_out[...] = sum_over(part_b, n_grid, slab, lambda j: (me, j), b_send, b_recv)
-    out_copy.wait()
-
-
-def small_kernel(sizes, f_in, total_in, f_out, projected_out, residual_out, out_sem):
-    nb, bands, width, cells = sizes
-    out_copy = pltpu.make_async_copy(f_in, f_out, out_sem)
-    out_copy.start()
-    me = lax.axis_index("band")
-    total = total_in[...] * (1.0 / cells)
+    total = sum_over(part_b, n_grid, slab, lambda j: (me, j), b_send, b_recv) * (1.0 / cells)
     groups = [total] + [
         pltpu.roll(total, width - 2 * bands * group, 1) for group in range(1, bands // 8 + 1)
     ]
@@ -331,14 +349,18 @@
     work = jnp.concatenate(groups[:-1], axis=0)
     unit = jnp.where(lane_of == row_of + 2 * bands, 1.0, 0.0)
     work = jnp.where(lane_of < 2 * bands, work, unit)
+    columns = [jnp.broadcast_to(work[:, k : k + 1], (bands, ny)) for k in range(bands)]
+    lane_tile = lax.broadcasted_iota(jnp.int32, (bands, ny), 0)
+    pivots = jnp.ones((bands, ny), jnp.float32)
     for k in range(bands):
-        pivot = work[k : k + 1, k : k + 1]
-        inverse = lax.rsqrt(pivot)
-        inverse = inverse * (1.5 - 0.5 * pivot * inverse * inverse)
-        row = work[k : k + 1, :] * inverse
-        factor_column = work[:, k : k + 1] * inverse
-        below = work - factor_column * row
-        work = jnp.where(row_of > k, below, jnp.where(row_of == k, row, work))
+        own_column = columns[k]
+        pivot = jnp.broadcast_to(own_column[k : k + 1], (bands, ny))
+        pivots = jnp.where(lane_tile == k, pivot, pivots)
+        multiplier = jnp.where(lane_tile > k, own_column, 0.0) / pivot
+        work = work - jnp.concatenate([multiplier] * (width // ny), axis=1) * work[k : k + 1]
+        for j in range(k + 1, bands):
+            columns[j] = columns[j] - multiplier * own_column[j : j + 1]
+    work = work / jnp.sqrt(jnp.concatenate([pivots] * (width // ny), axis=1))
     coefficients = jnp.where(lane_of < bands, pltpu.roll(work, width - bands, 1), 0.0)
     inverse_factor = jnp.where(lane_of < bands, pltpu.roll(work, width - 2 * bands, 1), 0.0)
     projected = lax.dot_general(
@@ -374,16 +396,18 @@
         def field(halo):
             return pltpu.VMEM((nb, rows + 2 * halo * nx, ny), f32)
 
-        shares, total = pl.pallas_call(
-            functools.partial(kernel, (nb, nz, nx, n_band, n_grid, share, width)),
+        filtered, projected, residual = pl.pallas_call(
+            functools.partial(kernel, (nb, nz, nx, n_band, n_grid, share, width, cells)),
             out_shape=(
                 jax.ShapeDtypeStruct((nb, rows, ny), f32),
-                jax.ShapeDtypeStruct((8, width), f32),
+                jax.ShapeDtypeStruct((nb, bands), f32),
+                jax.ShapeDtypeStruct((nb,), f32),
             ),
             in_specs=[pl.BlockSpec(memory_space=pltpu.HBM)] * 2,
             out_specs=(
                 pl.BlockSpec(memory_space=pltpu.HBM),
                 pl.BlockSpec(memory_space=pltpu.VMEM),
+                pl.BlockSpec(memory_space=pltpu.SMEM),
             ),
             scratch_shapes=[
                 field(4),
@@ -409,25 +433,6 @@
                 collective_id=0, has_side_effects=True, vmem_limit_bytes=VMEM_LIMIT
             ),
         )(trial_bands.reshape(nb, rows, ny), potential.reshape(rows, ny))
-        filtered, projected, residual = pl.pallas_call(
-            functools.partial(small_kernel, (nb, bands, width, cells)),
-            out_shape=(
-                jax.ShapeDtypeStruct((nb, rows, ny), f32),
-                jax.ShapeDtypeStruct((nb, bands), f32),
-                jax.ShapeDtypeStruct((nb,), f32),
-            ),
-            in_specs=[
-                pl.BlockSpec(memory_space=pl.ANY),
-                pl.BlockSpec(memory_space=pltpu.VMEM),
-            ],
-            out_specs=(
-                pl.BlockSpec(memory_space=pltpu.HBM),
-                pl.BlockSpec(memory_space=pltpu.VMEM),
-                pl.BlockSpec(memory_space=pltpu.SMEM),
-            ),
-            scratch_shapes=[pltpu.SemaphoreType.DMA],
-            compiler_params=pltpu.CompilerParams(vmem_limit_bytes=VMEM_LIMIT),
-        )(shares, total)
         return filtered.reshape(nb, nz, nx, ny), projected, residual
 
     return jax.shard_map(

time: 52.4 us -> 45 us (0.86)
  Pallas kernels: 51.6 us -> 41.3 us
  local copies, waits for them, and re-layouts: 0 us -> 2.9 us
    pallas_call x1 -> x0, Pallas kernels: 12.3 us -> none  [on_device(): pl.pallas_call(functools.partial(small_kernel, (nb, bands, width, cells))...]
    unnamed x0 -> x7, local copies, waits for them, and re-layouts: none -> 2.9 us
    pallas_call x1, Pallas kernels: 39.3 us -> 41.3 us  [on_device(): pl.pallas_call(functools.partial(kernel, (nb, nz, nx, n_band, n_grid, sha...]
where the time goes in v3:
time: 45 us; the launch traced here: 44.9 us
  Pallas kernels  41.3 us (92%)
  local copies, waits for them, and re-layouts  2.9 us (6%)
  between operations  0.65 us (1%)
    pallas_call x1, Pallas kernels, on_device(): pl.pallas_call(functools.partial(kernel, (nb, nz, nx, n_band, n_grid, sha...  41.3 us
    unnamed x7, local copies, waits for them, and re-layouts  2.9 us

profile of v3, /device:TPU:0, one launch (start us, length us, event | category | flops | bytes accessed | tf_op | source)
XLA Modules:
  0.0 44.9 jit_solution(3305869658028265054)
XLA Ops:
  0.6 41.3 %shard_map.49 = (f32[2,320,128]{2,1,0:T(8,128)}, f32[2,16]{1,0:T(2,128)}, f32[2]{0:T(128)}) custom-call(f32[2,320,128]{2,1,0:T(8,128)} %bitcast.4, f32[320,128]{1,0:T(8,128)} %bitcast.5), custom_call_target="tpu_custom_call" | custom-call | tf_op jit(solution)/shard_map/pallas_call | solution.py:399
  42.0 0.0 copy-start
  42.0 1.7 %copy.8 = f32[2,10,32,128]{3,2,1,0:T(8,128)} copy(f32[2,10,32,128]{3,2,1,0:T(8,128)} %bitcast.3) | data formatting | bytes 655360
  43.7 0.0 copy-done
  43.7 0.0 copy-start.1
  43.7 0.6 %copy.9 = f32[2,16]{1,0:T(2,128)} copy(f32[2,16]{1,0:T(2,128)S(1)} %copy-done) | data formatting | bytes 256
  44.3 0.1 copy-done.1
  44.4 0.5 %copy.10 = f32[2]{0:T(128)} copy(f32[2]{0:T(128)S(1)} %copy-done.1) | data formatting | bytes 16
Async XLA Ops:
  42.0 1.7 %copy-start = (f32[2,16]{1,0:T(2,128)S(1)}, f32[2,16]{1,0:T(2,128)}, u32[]{:S(2)}) copy-start(f32[2,16]{1,0:T(2,128)} %get-tuple-element.13) | copy-start | bytes 388
  43.7 0.7 %copy-start.1 = (f32[2]{0:T(128)S(1)}, f32[2]{0:T(128)}, u32[]{:S(2)}) copy-start(f32[2]{0:T(128)} %get-tuple-element.14) | copy-start | bytes 28

commit v4 on v3

--- a/solution.py
+++ b/solution.py
@@ -102,44 +102,27 @@
             device_id_type=MESH,
         )
 
-    def up(index, band, src, first, dst, depth):
-        return halo_copy(
-            2 * (nb * index + band),
-            src.at[band, pl.ds((first + nz - depth) * nx, depth * nx)],
-            dst.at[band, pl.ds(0, depth * nx)],
+    def swap(index, src, first, dst, depth):
+        up = halo_copy(
+            2 * index,
+            src.at[:, pl.ds((first + nz - depth) * nx, depth * nx)],
+            dst.at[:, pl.ds(0, depth * nx)],
             right,
         )
-
-    def down(index, band, src, first, dst, depth):
-        return halo_copy(
-            2 * (nb * index + band) + 1,
-            src.at[band, pl.ds(first * nx, depth * nx)],
-            dst.at[band, pl.ds((nz + depth) * nx, depth * nx)],
+        down = halo_copy(
+            2 * index + 1,
+            src.at[:, pl.ds(first * nx, depth * nx)],
+            dst.at[:, pl.ds((nz + depth) * nx, depth * nx)],
             left,
         )
-
-    def swap(index, band, src, first, dst, depth):
-        return [up(index, band, src, first, dst, depth), down(index, band, src, first, dst, depth)]
-
-    def swap_x(band):
-        return swap(0, band, x_hbm, 0, x0, 4)
-
-    def swap_2(band):
-        return swap(1, band, y2, 4, y2, 4)
-
-    def swap_4(band):
-        return swap(2, band, y4, 2, y4, 2)
-
-    def each_band(body):
-        def step(band, carry):
-            body(band)
-            return carry
-
-        lax.fori_loop(0, nb, step, 0)
-
+        return [up, down]
+
+    swap_x = swap(0, x_hbm, 0, x0, 4)
+    swap_2 = swap(1, y2, 4, y2, 4)
+    swap_4 = swap(2, y4, 2, y4, 2)
     swap_v = [
-        halo_copy(6 * nb, v_hbm.at[pl.ds((nz - 2) * nx, 2 * nx)], vp.at[pl.ds(0, 2 * nx)], right),
-        halo_copy(6 * nb + 1, v_hbm.at[pl.ds(0, 2 * nx)], vp.at[pl.ds((nz + 2) * nx, 2 * nx)], left),
+        halo_copy(6, v_hbm.at[pl.ds((nz - 2) * nx, 2 * nx)], vp.at[pl.ds(0, 2 * nx)], right),
+        halo_copy(7, v_hbm.at[pl.ds(0, 2 * nx)], vp.at[pl.ds((nz + 2) * nx, 2 * nx)], left),
     ]
 
     def start_all(copies):
@@ -151,38 +134,39 @@
             copy.wait()
 
     start_all(swap_v)
-    each_band(lambda band: start_all(swap_x(band)))
+    start_all(swap_x)
 
     steps = filter_steps()
 
-    def planes(band, pieces, src, src_halo, dsts, scale, center, prev=None, prev_halo=0, weight=0.0):
-        lo, hi = pieces[0]
-        pairs = (hi - lo) // 2
-        jump = pieces[-1][0] - hi
-
-        def at(ref, halo, plane):
+    def planes(firsts, depth, src, src_halo, dsts, scale, center, prev=None, prev_halo=0, weight=0.0):
+        def at(ref, band, halo, plane):
             return ref[band, pl.ds(pl.multiple_of((plane + halo) * nx, nx), nx), :]
 
-        def body(step, carry):
-            first = lo + 2 * step + (step // pairs) * jump
-            for plane in (first, first + 1):
-                local = vp[pl.ds(pl.multiple_of((plane + 2) * nx, nx), nx), :]
-                local = (local + (3.75 - center)) * scale
-                here = at(src, src_halo, plane)
-                near = at(src, src_halo, plane - 1) + at(src, src_halo, plane + 1)
-                far = at(src, src_halo, plane - 2) + at(src, src_halo, plane + 2)
+        def one(plane):
+            local = vp[pl.ds(pl.multiple_of((plane + 2) * nx, nx), nx), :]
+            local = (local + (3.75 - center)) * scale
+            for band in range(nb):
+                here = at(src, band, src_halo, plane)
+                near = at(src, band, src_halo, plane - 1) + at(src, band, src_halo, plane + 1)
+                far = at(src, band, src_halo, plane - 2) + at(src, band, src_halo, plane + 2)
                 near += pltpu.roll(here, 1, 0) + pltpu.roll(here, nx - 1, 0)
                 far += pltpu.roll(here, 2, 0) + pltpu.roll(here, nx - 2, 0)
                 near += pltpu.roll(here, 1, 1) + pltpu.roll(here, ny - 1, 1)
                 far += pltpu.roll(here, 2, 1) + pltpu.roll(here, ny - 2, 1)
                 value = local * here - near * (scale * 2.0 / 3.0) + far * (scale / 24.0)
                 if prev is not None:
-                    value = value - weight * at(prev, prev_halo, plane)
+                    value = value - weight * at(prev, band, prev_halo, plane)
                 for dst, halo in dsts:
                     dst[band, pl.ds(pl.multiple_of((plane + halo) * nx, nx), nx), :] = value
-            return carry
-
-        lax.fori_loop(0, pairs * len(pieces), body, 0)
+
+        def body(step, carry):
+            for first in firsts:
+                for offset in range(group):
+                    one(first + step * group + offset)
+            return carry
+
+        group = 3 if depth % 3 == 0 else 2
+        lax.fori_loop(0, depth // group, body, 0)
 
     step_1 = functools.partial(planes, src=x0, src_halo=4, dsts=[(y1, 2)], scale=steps[0][0], center=CENTER)
     step_2 = functools.partial(
@@ -204,27 +188,50 @@
         f_share[:, rows:, :] = jnp.zeros((nb, padded - rows, ny), jnp.float32)
         image[:, rows:, :] = jnp.zeros((nb, padded - rows, ny), jnp.float32)
 
-    def to_band(band, src, dst, send, recv, d):
-        partner = lax.rem(me + d, n_band)
+    half = n_band // 2
+    side = me // half
+
+    def far_partner(d):
+        return (1 - side) * half + lax.rem(me + d, half)
+
+    def near_partner(d):
+        return side * half + lax.rem(me + d, half)
+
+    def to_band(partner, src, dst, send, recv):
         return pltpu.make_async_remote_copy(
-            src_ref=src.at[band, pl.ds(pl.multiple_of(partner * share, 8), share)],
-            dst_ref=dst.at[me, band],
-            send_sem=send.at[band, d],
-            recv_sem=recv.at[band, n_band - d],
+            src_ref=src.at[:, pl.ds(pl.multiple_of(partner * share, 8), share)],
+            dst_ref=dst.at[me],
+            send_sem=send.at[partner],
+            recv_sem=recv.at[me],
             device_id=(partner, slab),
             device_id_type=MESH,
         )
 
-    def start_band(band, *args):
+    def from_band(partner, src, dst, send, recv):
+        return pltpu.make_async_remote_copy(
+            src_ref=src.at[:, pl.ds(pl.multiple_of(partner * share, 8), share)],
+            dst_ref=dst.at[partner],
+            send_sem=send.at[partner],
+            recv_sem=recv.at[partner],
+            device_id=(partner, slab),
+            device_id_type=MESH,
+        )
+
+    def start_band(*args):
+        def far(d, carry):
+            to_band(far_partner(d), *args).start()
+            return carry
+
+        def near(d, carry):
+            to_band(near_partner(d), *args).start()
+            return carry
+
+        lax.fori_loop(0, half, far, 0)
+        lax.fori_loop(1, half, near, 0)
+
+    def wait_band(*args):
         def body(d, carry):
-            to_band(band, *args, d).start()
-            return carry
-
-        lax.fori_loop(1, n_band, body, 0)
-
-    def wait_band(band, *args):
-        def body(d, carry):
-            to_band(band, *args, d).wait()
+            from_band(lax.rem(me + d, n_band), *args).wait()
             return carry
 
         lax.fori_loop(1, n_band, body, 0)
@@ -232,41 +239,28 @@
     f_route = (f_share, f_all, f_send, f_recv)
     h_route = (image, h_all, h_send, h_recv)
 
-    inner = [(2, nz - 2)]
-    rim = [(0, 2), (nz - 2, nz)]
-    halo_rim = [(-2, 2), (nz - 2, nz + 2)]
-
-    def to_y2(band):
-        wait_all(swap_x(band))
-        step_1(band, halo_rim)
-        step_2(band, [(0, 4), (nz - 4, nz)])
-        start_all(swap_2(band))
-        if nz > 8:
-            step_2(band, [(4, nz - 4)])
-
-    def to_y4(band):
-        step_3(band, inner)
-        wait_all(swap_2(band))
-        step_3(band, halo_rim)
-        step_4(band, rim)
-        start_all(swap_4(band))
-        step_4(band, inner)
-        start_band(band, *f_route)
-
-    def to_image(band):
-        last(band, inner)
-        wait_all(swap_4(band))
-        last(band, rim)
-        start_band(band, *h_route)
-
     wait_all(own)
-    each_band(lambda band: step_1(band, inner))
+    step_1((2,), nz - 4)
     wait_all(swap_v)
-    each_band(to_y2)
-    each_band(to_y4)
+    wait_all(swap_x)
+    step_1((-2, nz - 2), 4)
+    step_2((0, nz - 4), 4)
+    start_all(swap_2)
+    if nz > 8:
+        step_2((4,), nz - 8)
+    step_3((2,), nz - 4)
+    wait_all(swap_2)
+    step_3((-2, nz - 2), 4)
+    step_4((0, nz - 2), 2)
+    start_all(swap_4)
+    step_4((2,), nz - 4)
+    start_band(*f_route)
     out_copy = pltpu.make_async_copy(f_share.at[:, pl.ds(0, rows)], f_out, local_sem.at[2])
     out_copy.start()
-    each_band(to_image)
+    last((2,), nz - 4)
+    wait_all(swap_4)
+    last((0, nz - 2), 2)
+    start_band(*h_route)
 
     own_rows = pl.ds(pl.multiple_of(me * share, 8), share)
     f_all[me] = f_share[:, own_rows, :]
@@ -291,8 +285,10 @@
                 preferred_element_type=jnp.float32,
             )
 
-        return lax.fori_loop(0, share // 8, body, jnp.zeros((stretched, stretched), jnp.float32))
-
+        return lax.fori_loop(0, share // 8, body, zero, unroll=unrolled)
+
+    zero = jnp.zeros((stretched, stretched), jnp.float32)
+    unrolled = share // 8 if stretched <= 128 else 1
     column = lax.broadcasted_iota(jnp.int32, (stretched, width), 0) // 8
     lane = lax.broadcasted_iota(jnp.int32, (stretched, width), 1)
 
@@ -301,9 +297,9 @@
         pick = jnp.where(column + offset == lane, 1.0, 0.0)
         return jnp.dot(products, pick, precision=HIGHEST, preferred_element_type=jnp.float32)
 
-    each_band(lambda band: wait_band(band, *f_route))
+    wait_band(*f_route)
     top = folded(gram(f_all), 0)
-    each_band(lambda band: wait_band(band, *h_route))
+    wait_band(*h_route)
     top = top + folded(gram(h_all), bands)
     whole = h_all[...]
     squares = (whole * whole).sum(axis=2).reshape(bands, ny)
@@ -422,10 +418,10 @@
                 pltpu.VMEM((n_band, nb, share, ny), f32),
                 pltpu.VMEM((n_band, 8, width), f32),
                 pltpu.VMEM((n_grid, 8, width), f32),
-                pltpu.SemaphoreType.DMA((6 * nb + 2,)),
-                pltpu.SemaphoreType.DMA((6 * nb + 2,)),
+                pltpu.SemaphoreType.DMA((8,)),
+                pltpu.SemaphoreType.DMA((8,)),
             ]
-            + [pltpu.SemaphoreType.DMA((nb, n_band))] * 4
+            + [pltpu.SemaphoreType.DMA((n_band,))] * 4
             + [pltpu.SemaphoreType.DMA((n_band,))] * 2
             + [pltpu.SemaphoreType.DMA((n_grid,))] * 2
             + [pltpu.SemaphoreType.DMA((3,))],

time: 45 us -> 46.7 us (1.038)
  Pallas kernels: 41.3 us -> 43 us
    pallas_call x1, Pallas kernels: 41.3 us -> 43 us  [on_device(): pl.pallas_call(functools.partial(kernel, (nb, nz, nx, n_band, n_grid, sha...]
where the time goes in v4:
time: 46.7 us; the launch traced here: 46.5 us
  Pallas kernels  43 us (92%)
  local copies, waits for them, and re-layouts  2.9 us (6%)
  between operations  0.65 us (1%)
    pallas_call x1, Pallas kernels, on_device(): pl.pallas_call(functools.partial(kernel, (nb, nz, nx, n_band, n_grid, sha...  43 us
    unnamed x7, local copies, waits for them, and re-layouts  2.9 us

profile of v4, /device:TPU:0, one launch (start us, length us, event | category | flops | bytes accessed | tf_op | source)
XLA Modules:
  0.0 46.5 jit_solution(15422162011939995390)
XLA Ops:
  0.6 43.0 %shard_map.49 = (f32[2,320,128]{2,1,0:T(8,128)}, f32[2,16]{1,0:T(2,128)}, f32[2]{0:T(128)}) custom-call(f32[2,320,128]{2,1,0:T(8,128)} %bitcast.4, f32[320,128]{1,0:T(8,128)} %bitcast.5), custom_call_target="tpu_custom_call" | custom-call | tf_op jit(solution)/shard_map/pallas_call | solution.py:395
  43.6 0.0 copy-start
  43.6 1.7 %copy.8 = f32[2,10,32,128]{3,2,1,0:T(8,128)} copy(f32[2,10,32,128]{3,2,1,0:T(8,128)} %bitcast.3) | data formatting | bytes 655360
  45.4 0.0 copy-done
  45.4 0.0 copy-start.1
  45.4 0.6 %copy.9 = f32[2,16]{1,0:T(2,128)} copy(f32[2,16]{1,0:T(2,128)S(1)} %copy-done) | data formatting | bytes 256
  45.9 0.1 copy-done.1
  46.0 0.5 %copy.10 = f32[2]{0:T(128)} copy(f32[2]{0:T(128)S(1)} %copy-done.1) | data formatting | bytes 16
Async XLA Ops:
  43.6 1.7 %copy-start = (f32[2,16]{1,0:T(2,128)S(1)}, f32[2,16]{1,0:T(2,128)}, u32[]{:S(2)}) copy-start(f32[2,16]{1,0:T(2,128)} %get-tuple-element.13) | copy-start | bytes 388
  45.4 0.7 %copy-start.1 = (f32[2]{0:T(128)S(1)}, f32[2]{0:T(128)}, u32[]{:S(2)}) copy-start(f32[2]{0:T(128)} %get-tuple-element.14) | copy-start | bytes 28

commit v5 on v3

--- a/solution.py
+++ b/solution.py
@@ -32,33 +32,28 @@
     x_hbm,
     v_hbm,
     f_out,
-    projected_out,
-    residual_out,
+    total_out,
     x0,
     vp,
     y1,
     y2,
     y3,
     y4,
-    image,
-    f_share,
-    f_all,
-    h_all,
+    shares,
+    gathered,
     part_a,
     part_b,
     halo_send,
     halo_recv,
-    f_send,
-    f_recv,
-    h_send,
-    h_recv,
+    share_send,
+    share_recv,
     a_send,
     a_recv,
     b_send,
     b_recv,
     local_sem,
 ):
-    nb, nz, nx, n_band, n_grid, share, width, cells = sizes
+    nb, nz, nx, n_band, n_grid, share, width = sizes
     rows = nz * nx
     bands = nb * n_band
     me = lax.axis_index("band")
@@ -154,6 +149,8 @@
     each_band(lambda band: start_all(swap_x(band)))
 
     steps = filter_steps()
+
+    f_share, image = shares.at[0], shares.at[1]
 
     def planes(band, pieces, src, src_halo, dsts, scale, center, prev=None, prev_halo=0, weight=0.0):
         lo, hi = pieces[0]
@@ -201,36 +198,32 @@
 
     padded = share * n_band
     if padded != rows:
-        f_share[:, rows:, :] = jnp.zeros((nb, padded - rows, ny), jnp.float32)
-        image[:, rows:, :] = jnp.zeros((nb, padded - rows, ny), jnp.float32)
-
-    def to_band(band, src, dst, send, recv, d):
+        shares[:, :, rows:, :] = jnp.zeros((2, nb, padded - rows, ny), jnp.float32)
+
+    def to_band(kind, band, d):
         partner = lax.rem(me + d, n_band)
         return pltpu.make_async_remote_copy(
-            src_ref=src.at[band, pl.ds(pl.multiple_of(partner * share, 8), share)],
-            dst_ref=dst.at[me, band],
-            send_sem=send.at[band, d],
-            recv_sem=recv.at[band, n_band - d],
+            src_ref=shares.at[kind, band, pl.ds(pl.multiple_of(partner * share, 8), share)],
+            dst_ref=gathered.at[kind, me, band],
+            send_sem=share_send.at[kind, band, d],
+            recv_sem=share_recv.at[kind, band, n_band - d],
             device_id=(partner, slab),
             device_id_type=MESH,
         )
 
-    def start_band(band, *args):
+    def start_band(kind, band):
         def body(d, carry):
-            to_band(band, *args, d).start()
+            to_band(kind, band, d).start()
             return carry
 
         lax.fori_loop(1, n_band, body, 0)
 
-    def wait_band(band, *args):
+    def wait_band(kind, band):
         def body(d, carry):
-            to_band(band, *args, d).wait()
+            to_band(kind, band, d).wait()
             return carry
 
         lax.fori_loop(1, n_band, body, 0)
-
-    f_route = (f_share, f_all, f_send, f_recv)
-    h_route = (image, h_all, h_send, h_recv)
 
     inner = [(2, nz - 2)]
     rim = [(0, 2), (nz - 2, nz)]
@@ -251,13 +244,13 @@
         step_4(band, rim)
         start_all(swap_4(band))
         step_4(band, inner)
-        start_band(band, *f_route)
+        start_band(0, band)
 
     def to_image(band):
         last(band, inner)
         wait_all(swap_4(band))
         last(band, rim)
-        start_band(band, *h_route)
+        start_band(1, band)
 
     wait_all(own)
     each_band(lambda band: step_1(band, inner))
@@ -269,8 +262,8 @@
     each_band(to_image)
 
     own_rows = pl.ds(pl.multiple_of(me * share, 8), share)
-    f_all[me] = f_share[:, own_rows, :]
-    h_all[me] = image[:, own_rows, :]
+    for kind in range(2):
+        gathered[kind, me] = shares[kind, :, own_rows, :]
 
     stretched = bands * 8
     same = (
@@ -278,14 +271,15 @@
         == lax.broadcasted_iota(jnp.int32, (stretched, stretched), 1) % 8
     )
 
-    def gram(ref):
+    def gram(kind):
         def tile(of, t):
-            return of[:, :, pl.ds(pl.multiple_of(8 * t, 8), 8), :].reshape(stretched, ny)
+            part = gathered[of, :, :, pl.ds(pl.multiple_of(8 * t, 8), 8), :]
+            return part.reshape(stretched, ny)
 
         def body(t, total):
             return total + lax.dot_general(
-                tile(f_all, t),
-                tile(ref, t),
+                tile(0, t),
+                tile(kind, t),
                 CONTRACT_LANES,
                 precision=HIGHEST,
                 preferred_element_type=jnp.float32,
@@ -301,11 +295,12 @@
         pick = jnp.where(column + offset == lane, 1.0, 0.0)
         return jnp.dot(products, pick, precision=HIGHEST, preferred_element_type=jnp.float32)
 
-    each_band(lambda band: wait_band(band, *f_route))
-    top = folded(gram(f_all), 0)
-    each_band(lambda band: wait_band(band, *h_route))
-    top = top + folded(gram(h_all), bands)
-    whole = h_all[...]
+    def one_kind(kind, top):
+        each_band(lambda band: wait_band(kind, band))
+        return top + folded(gram(kind), kind * bands)
+
+    top = lax.fori_loop(0, 2, one_kind, jnp.zeros((bands, width), jnp.float32))
+    whole = gathered[1]
     squares = (whole * whole).sum(axis=2).reshape(bands, ny)
     norm_lane = lax.broadcasted_iota(jnp.int32, (bands, width), 1) - 2 * bands * (bands // 8)
     norm_row = lax.broadcasted_iota(jnp.int32, (bands, width), 0)
@@ -340,7 +335,16 @@
         return jnp.sum(part[...], axis=0)
 
     part_b[slab] = sum_over(part_a, n_band, me, lambda j: (j, slab), a_send, a_recv)
-    total = sum_over(part_b, n_grid, slab, lambda j: (me, j), b_send, b_recv) * (1.0 / cells)
+    total_out[...] = sum_over(part_b, n_grid, slab, lambda j: (me, j), b_send, b_recv)
+    out_copy.wait()
+
+
+def small_kernel(sizes, f_in, total_in, f_out, projected_out, residual_out, out_sem):
+    nb, bands, width, ny, cells = sizes
+    out_copy = pltpu.make_async_copy(f_in, f_out, out_sem)
+    out_copy.start()
+    me = lax.axis_index("band")
+    total = total_in[...] * (1.0 / cells)
     groups = [total] + [
         pltpu.roll(total, width - 2 * bands * group, 1) for group in range(1, bands // 8 + 1)
     ]
@@ -396,18 +400,16 @@
         def field(halo):
             return pltpu.VMEM((nb, rows + 2 * halo * nx, ny), f32)
 
-        filtered, projected, residual = pl.pallas_call(
-            functools.partial(kernel, (nb, nz, nx, n_band, n_grid, share, width, cells)),
+        f_held, total = pl.pallas_call(
+            functools.partial(kernel, (nb, nz, nx, n_band, n_grid, share, width)),
             out_shape=(
                 jax.ShapeDtypeStruct((nb, rows, ny), f32),
-                jax.ShapeDtypeStruct((nb, bands), f32),
-                jax.ShapeDtypeStruct((nb,), f32),
+                jax.ShapeDtypeStruct((8, width), f32),
             ),
             in_specs=[pl.BlockSpec(memory_space=pltpu.HBM)] * 2,
             out_specs=(
                 pl.BlockSpec(memory_space=pltpu.HBM),
                 pl.BlockSpec(memory_space=pltpu.VMEM),
-                pl.BlockSpec(memory_space=pltpu.SMEM),
             ),
             scratch_shapes=[
                 field(4),
@@ -416,16 +418,14 @@
                 field(4),
                 field(2),
                 field(2),
-                pltpu.VMEM((nb, share * n_band, ny), f32),
-                pltpu.VMEM((nb, share * n_band, ny), f32),
-                pltpu.VMEM((n_band, nb, share, ny), f32),
-                pltpu.VMEM((n_band, nb, share, ny), f32),
+                pltpu.VMEM((2, nb, share * n_band, ny), f32),
+                pltpu.VMEM((2, n_band, nb, share, ny), f32),
                 pltpu.VMEM((n_band, 8, width), f32),
                 pltpu.VMEM((n_grid, 8, width), f32),
                 pltpu.SemaphoreType.DMA((6 * nb + 2,)),
                 pltpu.SemaphoreType.DMA((6 * nb + 2,)),
             ]
-            + [pltpu.SemaphoreType.DMA((nb, n_band))] * 4
+            + [pltpu.SemaphoreType.DMA((2, nb, n_band))] * 2
             + [pltpu.SemaphoreType.DMA((n_band,))] * 2
             + [pltpu.SemaphoreType.DMA((n_grid,))] * 2
             + [pltpu.SemaphoreType.DMA((3,))],
@@ -433,6 +433,25 @@
                 collective_id=0, has_side_effects=True, vmem_limit_bytes=VMEM_LIMIT
             ),
         )(trial_bands.reshape(nb, rows, ny), potential.reshape(rows, ny))
+        filtered, projected, residual = pl.pallas_call(
+            functools.partial(small_kernel, (nb, bands, width, ny, cells)),
+            out_shape=(
+                jax.ShapeDtypeStruct((nb, rows, ny), f32),
+                jax.ShapeDtypeStruct((nb, bands), f32),
+                jax.ShapeDtypeStruct((nb,), f32),
+            ),
+            in_specs=[
+                pl.BlockSpec(memory_space=pltpu.HBM),
+                pl.BlockSpec(memory_space=pltpu.VMEM),
+            ],
+            out_specs=(
+                pl.BlockSpec(memory_space=pltpu.HBM),
+                pl.BlockSpec(memory_space=pltpu.VMEM),
+                pl.BlockSpec(memory_space=pltpu.SMEM),
+            ),
+            scratch_shapes=[pltpu.SemaphoreType.DMA],
+            compiler_params=pltpu.CompilerParams(vmem_limit_bytes=VMEM_LIMIT),
+        )(f_held, total)
         return filtered.reshape(nb, nz, nx, ny), projected, residual
 
     return jax.shard_map(

time: 45 us -> 54 us (1.20)
  Pallas kernels: 41.3 us -> 53.2 us
  local copies, waits for them, and re-layouts: 2.9 us -> 0 us
    pallas_call x0 -> x1, Pallas kernels: none -> 12.3 us  [on_device(): pl.pallas_call(functools.partial(small_kernel, (nb, bands, width, ny, cel...]
    unnamed x7 -> x0, local copies, waits for them, and re-layouts: 2.9 us -> none
where the time goes in v5:
time: 54 us; the launch traced here: 53.8 us
  Pallas kernels  53.2 us (99%)
  between operations  0.64 us (1%)
    pallas_call x1, Pallas kernels, on_device(): pl.pallas_call(functools.partial(kernel, (nb, nz, nx, n_band, n_grid, sha...  40.9 us
    pallas_call x1, Pallas kernels, on_device(): pl.pallas_call(functools.partial(small_kernel, (nb, bands, width, ny, cel...  12.3 us

profile of v5, /device:TPU:0, one launch (start us, length us, event | category | flops | bytes accessed | tf_op | source)
XLA Modules:
  0.0 53.8 jit_solution(11973437075510052555)
XLA Ops:
  0.6 40.9 %shard_map.49 = (f32[2,320,128]{2,1,0:T(8,128)}, f32[8,128]{1,0:T(8,128)}) custom-call(f32[2,320,128]{2,1,0:T(8,128)} %bitcast.3, f32[320,128]{1,0:T(8,128)} %bitcast.4), custom_call_target="tpu_custom_call" | custom-call | tf_op jit(solution)/shard_map/pallas_call | solution.py:403
  41.5 12.3 %shard_map.50 = (f32[2,320,128]{2,1,0:T(8,128)}, f32[2,16]{1,0:T(2,128)}, f32[2]{0:T(128)}) custom-call(f32[2,320,128]{2,1,0:T(8,128)} %get-tuple-element.8.f_in, f32[8,128]{1,0:T(8,128)} %get-tuple-element.9.total_in), custom_call_target="tpu_custom_call" | custom-call | tf_op jit(solution)/shard_map/pallas_call | solution.py:436

commit v6 on v5

--- a/solution.py
+++ b/solution.py
@@ -117,7 +117,7 @@
         return [up(index, band, src, first, dst, depth), down(index, band, src, first, dst, depth)]
 
     def swap_x(band):
-        return swap(0, band, x_hbm, 0, x0, 4)
+        return swap(0, band, x0, 4, x0, 4)
 
     def swap_2(band):
         return swap(1, band, y2, 4, y2, 4)
@@ -133,8 +133,8 @@
         lax.fori_loop(0, nb, step, 0)
 
     swap_v = [
-        halo_copy(6 * nb, v_hbm.at[pl.ds((nz - 2) * nx, 2 * nx)], vp.at[pl.ds(0, 2 * nx)], right),
-        halo_copy(6 * nb + 1, v_hbm.at[pl.ds(0, 2 * nx)], vp.at[pl.ds((nz + 2) * nx, 2 * nx)], left),
+        halo_copy(6 * nb, vp.at[pl.ds(nz * nx, 2 * nx)], vp.at[pl.ds(0, 2 * nx)], right),
+        halo_copy(6 * nb + 1, vp.at[pl.ds(2 * nx, 2 * nx)], vp.at[pl.ds((nz + 2) * nx, 2 * nx)], left),
     ]
 
     def start_all(copies):
@@ -145,6 +145,7 @@
         for copy in copies:
             copy.wait()
 
+    wait_all(own)
     start_all(swap_v)
     each_band(lambda band: start_all(swap_x(band)))
 
@@ -252,7 +253,6 @@
         last(band, rim)
         start_band(1, band)
 
-    wait_all(own)
     each_band(lambda band: step_1(band, inner))
     wait_all(swap_v)
     each_band(to_y2)
@@ -339,9 +339,12 @@
     out_copy.wait()
 
 
-def small_kernel(sizes, f_in, total_in, f_out, projected_out, residual_out, out_sem):
+def small_kernel(sizes, f_in, total_in, f_out, projected_out, residual_out, f_held, out_sem):
     nb, bands, width, ny, cells = sizes
-    out_copy = pltpu.make_async_copy(f_in, f_out, out_sem)
+    in_copy = pltpu.make_async_copy(f_in, f_held, out_sem.at[0])
+    in_copy.start()
+    in_copy.wait()
+    out_copy = pltpu.make_async_copy(f_held, f_out, out_sem.at[1])
     out_copy.start()
     me = lax.axis_index("band")
     total = total_in[...] * (1.0 / cells)
@@ -449,7 +452,7 @@
                 pl.BlockSpec(memory_space=pltpu.VMEM),
                 pl.BlockSpec(memory_space=pltpu.SMEM),
             ),
-            scratch_shapes=[pltpu.SemaphoreType.DMA],
+            scratch_shapes=[pltpu.VMEM((nb, rows, ny), f32), pltpu.SemaphoreType.DMA((2,))],
             compiler_params=pltpu.CompilerParams(vmem_limit_bytes=VMEM_LIMIT),
         )(f_held, total)
         return filtered.reshape(nb, nz, nx, ny), projected, residual

time: 54 us -> 44.5 us (0.82)
  Pallas kernels: 53.2 us -> 43.6 us
    pallas_call x1, Pallas kernels: 12.3 us -> 2.96 us  [on_device(): pl.pallas_call(functools.partial(small_kernel, (nb, bands, width, ny, cel...]
where the time goes in v6:
time: 44.5 us; the launch traced here: 44.3 us
  Pallas kernels  43.6 us (98%)
  between operations  0.64 us (1%)
    pallas_call x1, Pallas kernels, on_device(): pl.pallas_call(functools.partial(kernel, (nb, nz, nx, n_band, n_grid, sha...  40.7 us
    pallas_call x1, Pallas kernels, on_device(): pl.pallas_call(functools.partial(small_kernel, (nb, bands, width, ny, cel...  2.96 us

profile of v6, /device:TPU:0, one launch (start us, length us, event | category | flops | bytes accessed | tf_op | source)
XLA Modules:
  0.0 44.3 jit_solution(17277527471085691725)
XLA Ops:
  0.6 40.7 %shard_map.49 = (f32[2,320,128]{2,1,0:T(8,128)}, f32[8,128]{1,0:T(8,128)}) custom-call(f32[2,320,128]{2,1,0:T(8,128)} %bitcast.3, f32[320,128]{1,0:T(8,128)} %bitcast.4), custom_call_target="tpu_custom_call" | custom-call | tf_op jit(solution)/shard_map/pallas_call | solution.py:406
  41.3 3.0 %shard_map.50 = (f32[2,320,128]{2,1,0:T(8,128)}, f32[2,16]{1,0:T(2,128)}, f32[2]{0:T(128)}) custom-call(f32[2,320,128]{2,1,0:T(8,128)} %get-tuple-element.8.f_in, f32[8,128]{1,0:T(8,128)} %get-tuple-element.9.total_in), custom_call_target="tpu_custom_call" | custom-call | tf_op jit(solution)/shard_map/pallas_call | solution.py:439

commit v7 on v6

--- a/solution.py
+++ b/solution.py
@@ -217,7 +217,8 @@
             to_band(kind, band, d).start()
             return carry
 
-        lax.fori_loop(1, n_band, body, 0)
+        lax.fori_loop(n_band // 2, n_band, body, 0)
+        lax.fori_loop(1, n_band // 2, body, 0)
 
     def wait_band(kind, band):
         def body(d, carry):

time: 44.5 us -> 44 us (0.989)
  Pallas kernels: 43.6 us -> 43.1 us
    pallas_call x1, Pallas kernels: 40.7 us -> 40.2 us  [on_device(): pl.pallas_call(functools.partial(kernel, (nb, nz, nx, n_band, n_grid, sha...]
where the time goes in v7:
time: 44 us; the launch traced here: 43.8 us
  Pallas kernels  43.1 us (98%)
  between operations  0.64 us (1%)
    pallas_call x1, Pallas kernels, on_device(): pl.pallas_call(functools.partial(kernel, (nb, nz, nx, n_band, n_grid, sha...  40.2 us
    pallas_call x1, Pallas kernels, on_device(): pl.pallas_call(functools.partial(small_kernel, (nb, bands, width, ny, cel...  2.96 us

profile of v7, /device:TPU:0, one launch (start us, length us, event | category | flops | bytes accessed | tf_op | source)
XLA Modules:
  0.0 43.8 jit_solution(4690815468045795549)
XLA Ops:
  0.6 40.2 %shard_map.49 = (f32[2,320,128]{2,1,0:T(8,128)}, f32[8,128]{1,0:T(8,128)}) custom-call(f32[2,320,128]{2,1,0:T(8,128)} %bitcast.3, f32[320,128]{1,0:T(8,128)} %bitcast.4), custom_call_target="tpu_custom_call" | custom-call | tf_op jit(solution)/shard_map/pallas_call | solution.py:407
  40.8 3.0 %shard_map.50 = (f32[2,320,128]{2,1,0:T(8,128)}, f32[2,16]{1,0:T(2,128)}, f32[2]{0:T(128)}) custom-call(f32[2,320,128]{2,1,0:T(8,128)} %get-tuple-element.8.f_in, f32[8,128]{1,0:T(8,128)} %get-tuple-element.9.total_in), custom_call_target="tpu_custom_call" | custom-call | tf_op jit(solution)/shard_map/pallas_call | solution.py:440
